TPU v7x, 256 devices: a whole 4x4x8 slice. The times are simulated.
256 devices in a mesh: prow: 32 (over z, y_hi, core), pcol: 8 (over y_lo, x).
Axes of the slice: x: 4, y: 4 (y_hi: 2, y_lo: 2; y = y_hi * 2 + y_lo), z: 8, core: 2. Of those that a mesh axis runs over, the one named last changes fastest.
Arguments:
- struct_rows: int32 [2, 80], replicated, may hold values from 0 to 127, as said below
- lpanel: float32 [2, 24576, 192], P(None, 'prow'), may hold values from -0.046875 to 0.046875
- ainv: float32 [24576, 24576], P('prow', 'pcol'), may hold values from -6 to 6
- dinv: float32 [2, 192, 192], replicated, may hold values from -6 to 6
Outputs:
- inv_row: float32 [2, 192, 24576], P(None, None, 'pcol')
- inv_diag: float32 [2, 192, 192], replicated
Inputs may be any that keep to these rules, and one draw needn't show every extreme that they name: `struct_rows`: each row lists 80 distinct block rows in increasing order; block rows 0 and 127 are always listed.
All inputs are finite; a program needn't handle non-finite values.
Results may differ from a plain program's by a relative error of at most 0.0001.
Values sent between devices are 32-bit elements; how exact they have to be, the bound alone decides.
No kernel may reach another device: no remote copies, remote signals or barrier semaphores. Data moves between devices by JAX's collectives and lax.ppermute only.
A program may use at most 64 MiB of HBM per device.

v0:
```python
import jax
import jax.numpy as jnp
from jax import lax
from jax.sharding import PartitionSpec as P


def from_root(block, axis, source):
    block = jnp.where(lax.axis_index(axis) == source, block, jnp.zeros_like(block))
    return lax.psum(block, axis)


def member_mask(struct_rows, block_ids, width):
    inside = jnp.any(struct_rows[:, :, None] == block_ids[None, None, :], axis=1)
    return jnp.repeat(inside.astype(jnp.float32), width, axis=1)


def local(struct_rows, lpanel, ainv, dinv):
    count_rows = lax.axis_size("prow")
    count_cols = lax.axis_size("pcol")
    row_index = lax.axis_index("prow")
    col_index = lax.axis_index("pcol")
    width = dinv.shape[1]
    rows_local = lpanel.shape[1]
    cols_local = ainv.shape[1]
    row_blocks = rows_local // width
    col_blocks = cols_local // width
    row_ids = row_index * row_blocks + jnp.arange(row_blocks, dtype=jnp.int32)
    col_ids = col_index * col_blocks + jnp.arange(col_blocks, dtype=jnp.int32)
    row_mask = member_mask(struct_rows, row_ids, width)
    col_mask = member_mask(struct_rows, col_ids, width)
    masked = lpanel * row_mask[:, :, None]
    lines = []
    for column in range(masked.shape[0]):
        partial_value = -lax.dot_general(
            masked[column],
            ainv,
            (((0,), (0,)), ((), ())),
            precision=lax.Precision.HIGHEST,
            preferred_element_type=jnp.float32,
        )
        summed = lax.psum(partial_value, "prow")
        lines.append(summed * col_mask[column][None, :])
    inv_row = jnp.stack(lines)
    per_col = count_rows // count_cols
    owner_col = row_index // per_col
    offset = row_index % per_col * rows_local
    own_rows = lax.dynamic_slice_in_dim(inv_row, offset, rows_local, 2)
    shared = from_root(own_rows, "pcol", owner_col)
    contrib = jnp.einsum(
        "kbr,krc->kbc",
        shared,
        masked,
        precision=lax.Precision.HIGHEST,
        preferred_element_type=jnp.float32,
    )
    diag_sum = lax.psum(contrib, "prow")
    inv_diag = dinv - diag_sum
    return (inv_row, inv_diag)


def solution(mesh):
    in_specs = (P(), P(None, "prow", None), P("prow", "pcol"), P())
    out_specs = (P(None, None, "pcol"), P())
    return jax.shard_map(local, mesh=mesh, in_specs=in_specs, out_specs=out_specs, check_vma=False)
```

profile of v0, /device:TPU:1, one launch (start us, length us, event | category | flops | bytes accessed | tf_op | source)
XLA Modules:
  0.0 671.2 jit_solution(2525035966288208881)
XLA Ops:
  7.2 0.0 all-reduce.9.cloned.1.call-start
  7.2 0.9 compare_reduce_fusion.1
  8.1 0.1 broadcast_in_dim.19
  8.2 0.1 mul.36
  8.3 1.4 broadcast_multiply_fusion
  9.6 0.0 copy-start
  9.6 9.9 %convolution_negate_fusion = f32[192,3072]{1,0:T(8,128)} fusion(f32[768,3072]{1,0:T(8,128)} %param.6, f32[2,768,192]{1,2,0:T(8,128)S(1)} %broadcast_multiply_fusion), kind=kOutput, calls=%fused_computation.3 | convolution fusion | flops 5436407808 | bytes 12386304 | tf_op jit(solution)/shard_map/dot_general | solution.py:34
  19.5 0.0 copy-done
  19.5 8.0 %convolution_negate_fusion.1 = f32[192,3072]{1,0:T(8,128)} fusion(f32[768,3072]{1,0:T(8,128)S(1)} %copy-done, f32[2,768,192]{1,2,0:T(8,128)S(1)} %broadcast_multiply_fusion), kind=kOutput, calls=%fused_computation.4 | convolution fusion | flops 5436407808 | bytes 12386304 | tf_op jit(solution)/shard_map/dot_general | solution.py:34
  27.5 0.0 all-reduce.9.cloned.1.call-update
  27.5 0.0 all-reduce.5.cloned.1.call-start
  27.6 0.6 copy-done.3
  28.2 0.2 compare_reduce_fusion
  28.4 0.1 broadcast_in_dim.20
  28.4 0.1 broadcast_in_dim.21
  28.5 0.1 broadcast_in_dim.22
  28.6 0.7 broadcast_in_dim.23
  29.3 286.1 %all-reduce.9.cloned.1.call-done = (f32[192,3072]{1,0:T(8,128)}, f32[192,3072]{1,0:T(8,128)}) async-done(((f32[192,3072]{1,0:T(8,128)}, f32[192,3072]{1,0:T(8,128)}), (f32[192,3072]{1,0:T(8,128)}, f32[192,3072]{1,0:T(8,128)})) %all-reduce.9.cloned.1.call-update) | async-done | bytes 4718608 | tf_op jit(solution)/shard_map/psum | solution.py:41
  315.4 2.9 multiply_bitcast_fusion
  318.3 0.0 copy-start.1
  318.3 1.4 copy-done.1
  319.7 1.1 fusion.1
  320.8 0.0 all-reduce.5.cloned.1.call-update
  320.9 0.0 all-reduce.7.cloned.1.call-start
  320.9 77.5 %all-reduce.5.cloned.1.call-done = f32[2,192,768]{2,1,0:T(8,128)} async-done(((f32[2,192,768]{2,1,0:T(8,128)}), f32[2,192,768]{2,1,0:T(8,128)}) %all-reduce.5.cloned.1.call-update) | async-done | bytes 1179664 | tf_op jit(solution)/shard_map/psum | solution.py:9
  398.4 3.3 fusion.2
  401.6 0.0 all-reduce.7.cloned.1.call-update
  401.6 0.0 copy-start.2
  401.7 4.3 pad_maximum_fusion
  406.0 256.9 %all-reduce.7.cloned.1.call-done = f32[2,192,192]{2,1,0:T(8,128)} async-done(((f32[2,192,192]{2,1,0:T(8,128)}), f32[2,192,192]{2,1,0:T(8,128)}) %all-reduce.7.cloned.1.call-update) | async-done | bytes 294928 | tf_op jit(solution)/shard_map/psum | solution.py:56
  662.9 0.0 copy-done.2
  662.9 1.8 sub.8
  (6 shorter events, 0.0 us)
Async XLA Ops:
  7.2 308.2 %all-reduce.9.cloned.1.call-start = ((), (), s32[]{:S(2)}) async-start(), calls=%async_computation.2 | async-start | bytes 9437184 | tf_op jit(solution)/shard_map/psum | solution.py:41
  9.6 9.9 %copy-start = (f32[768,3072]{1,0:T(8,128)S(1)}, f32[768,3072]{1,0:T(8,128)}, u32[]{:S(2)}) copy-start(f32[768,3072]{1,0:T(8,128)} %param.6) | copy-start | bytes 28311556
  27.5 0.7 copy-start.3
  27.5 370.8 %all-reduce.5.cloned.1.call-start = ((), (), s32[]{:S(2)}) async-start(), calls=%async_computation | async-start | bytes 2359296 | tf_op jit(solution)/shard_map/psum | solution.py:9
  318.3 1.4 copy-start.1
  320.9 342.0 %all-reduce.7.cloned.1.call-start = ((), (), s32[]{:S(2)}) async-start(), calls=%async_computation.1 | async-start | bytes 786432 | tf_op jit(solution)/shard_map/psum | solution.py:56
  401.6 261.2 %copy-start.2 = (f32[2,192,192]{2,1,0:T(8,128)S(1)}, f32[2,192,192]{2,1,0:T(8,128)}, u32[]{:S(2)}) copy-start(f32[2,192,192]{2,1,0:T(8,128)} %param.7) | copy-start | bytes 884740
Sparse Core Ops, SparseCore 0:
  27.6 287.7 all-reduce.8
  321.0 77.3 all-reduce.4
  401.8 261.0 all-reduce.6
where the time goes:
time: 672 us; the launch traced here: 671 us
  waiting for transfers between devices  621 us (92%)
  matrix products  21.1 us (3%)
  between operations  13.8 us (2%)
  other arithmetic  12.5 us (2%)
    psum x1, waiting for transfers between devices, local(): summed = lax.psum(partial_value, 'prow')  286 us
    psum x1, waiting for transfers between devices, local(): diag_sum = lax.psum(contrib, 'prow')  257 us
    psum x1, waiting for transfers between devices, from_root(): return lax.psum(block, axis)  77.5 us
    dot_general x2, matrix products, local(): lax.dot_general(masked[column], ainv, (((0,), (0,)), ((), ())), precision...  17.9 us
  transfers between devices with their start and end apart: 3, of which 3 were waited for; matrix products, arithmetic and copies ran while one was open for 1% of the time, Pallas kernels for 0%

commit v1 on v0

v1 whole, which is shorter than its diff:
```python
import functools

import jax
import jax.numpy as jnp
from jax import lax
from jax.experimental import pallas as pl
from jax.experimental.pallas import tpu as pltpu
from jax.sharding import PartitionSpec as P

AXES = ("prow", "pcol")
NZ, NYH, NC, NYL, NX = 8, 2, 2, 2, 4
REL = (4, 3, -3, 2, -2, 1, -1, 0)


def rank(z, yh, c, yl, x):
    return ((z * NYH + yh) * NC + c) * (NYL * NX) + yl * NX + x


def places():
    return [
        (z, yh, c, yl, x)
        for z in range(NZ)
        for yh in range(NYH)
        for c in range(NC)
        for yl in range(NYL)
        for x in range(NX)
    ]


def shift(value, dz=0, fz=0, fyh=0, fc=0, fyl=0, fx=0):
    perm = [
        (rank(z, yh, c, yl, x), rank(((z + dz) % NZ) ^ fz, yh ^ fyh, c ^ fc, yl ^ fyl, x ^ fx))
        for z, yh, c, yl, x in places()
    ]
    return lax.ppermute(value, AXES, perm)


def split(value):
    high = value.astype(jnp.bfloat16)
    low = (value - high.astype(jnp.float32)).astype(jnp.bfloat16)
    return high, low


def dot(a, b):
    return lax.dot_general(a, b, (((1,), (0,)), ((), ())), preferred_element_type=jnp.float32)


def product_kernel(meta, struct_ref, panel_ref, ainv_ref, out_ref, left_hl, left_h):
    width = out_ref.shape[1]

    @pl.when(pl.program_id(0) == 0)
    def _():
        listed = struct_ref[pl.ds(meta[0], 1), :]
        for i in range(panel_ref.shape[1] // width):
            hit = jnp.where(listed == meta[1] + i, -1.0, 0.0)
            sign = jnp.min(hit, axis=1, keepdims=True)
            block = (panel_ref[0, i * width : (i + 1) * width, :] * sign).T
            high, low = split(block)
            left_hl[:width, i * width : (i + 1) * width] = high
            left_hl[width:, i * width : (i + 1) * width] = low
            left_h[:, i * width : (i + 1) * width] = high

    high, low = split(ainv_ref[...])
    both = dot(left_hl[...], high)
    out_ref[0] = (both[width:] + dot(left_h[...], low)) + both[:width]


def product(meta, struct_rows, lpanel, ainv, first, count):
    _, rows, width = lpanel.shape
    cols = ainv.shape[1] // NZ
    return pl.pallas_call(
        product_kernel,
        out_shape=jax.ShapeDtypeStruct((count, width, cols), jnp.float32),
        grid_spec=pltpu.PrefetchScalarGridSpec(
            num_scalar_prefetch=1,
            grid=(count,),
            in_specs=[
                pl.BlockSpec(struct_rows.shape, lambda j, meta: (0, 0)),
                pl.BlockSpec((1, rows, width), lambda j, meta: (meta[0], 0, 0)),
                pl.BlockSpec((rows, cols), lambda j, meta: (0, meta[2 + first + j])),
            ],
            out_specs=pl.BlockSpec((1, width, cols), lambda j, meta: (j, 0, 0)),
            scratch_shapes=[
                pltpu.VMEM((2 * width, rows), jnp.bfloat16),
                pltpu.VMEM((width, rows), jnp.bfloat16),
            ],
        ),
        compiler_params=pltpu.CompilerParams(vmem_limit_bytes=24 * 1024 * 1024),
        cost_estimate=pl.CostEstimate(
            flops=6 * count * rows * width * cols, bytes_accessed=4 * count * rows * cols, transcendentals=0
        ),
    )(meta, struct_rows, lpanel, ainv)


def local(struct_rows, lpanel, ainv, dinv):
    row_index = lax.axis_index("prow")
    col_index = lax.axis_index("pcol")
    z = row_index // (NYH * NC)
    core = row_index % NC
    _, rows, width = lpanel.shape
    cols = ainv.shape[1]
    chunk = cols // NZ
    half = width // 2
    row_blocks = rows // width
    chunk_blocks = chunk // width
    owners = [(z + rel + NZ) % NZ for rel in REL]

    perm = []
    for pz, pyh, pc, pyl, px in places():
        q = pyl * NX + px
        z2, yh2, c2 = q >> 2, (q >> 1) & 1, q & 1
        dest_z = (pyh * NC + pc) * 2 + z2
        perm.append((rank(pz, pyh, pc, pyl, px), rank(dest_z, yh2, c2, pz // NX, pz % NX)))
    start = (col_index // 4) * chunk
    give = lax.dynamic_slice(lpanel, (col_index % 2, start, 0), (1, chunk, width))[0]
    facing = lax.ppermute(give, AXES, perm)

    def meta_of(k):
        return jnp.stack([k, row_index * row_blocks] + owners).astype(jnp.int32)

    other, own = meta_of(1 - core), meta_of(core)
    prod = functools.partial(product, struct_rows=struct_rows, lpanel=lpanel, ainv=ainv)
    cut = 3
    send_a = prod(other, first=0, count=cut)
    got_a = shift(send_a, fc=1)
    send_b = prod(other, first=cut, count=NZ - cut)
    got_b = shift(send_b, fc=1)
    own_a = prod(own, first=0, count=cut)
    own_b = prod(own, first=cut, count=NZ - cut)

    def part(rel):
        i = REL.index(rel)
        if i < cut:
            return own_a[i] + got_a[i]
        return own_b[i - cut] + got_b[i - cut]

    first = part(4)
    up = shift(first[:half], dz=1)
    down = shift(first[half:], dz=-1)
    p3, m3 = part(3), part(-3)
    send_up = jnp.concatenate([p3[:half] + up, p3[half:]])
    send_down = jnp.concatenate([m3[:half], m3[half:] + down])
    for d in (2, 1, 0):
        up = shift(send_up, dz=1)
        down = shift(send_down, dz=-1)
        if d:
            send_up = part(d) + up
            send_down = part(-d) + down
    mine = part(0) + up + down
    mine = mine + shift(mine, fyh=1)

    ids = (col_index * NZ + z) * chunk_blocks + jnp.arange(chunk_blocks, dtype=jnp.int32)
    listed = lax.dynamic_slice_in_dim(struct_rows, core, 1, 0)
    inside = jnp.any(listed[0][:, None] == ids[None, :], axis=0)
    col_mask = jnp.repeat(inside.astype(jnp.float32), width)
    mine = mine * col_mask[None, :]

    diag = lax.dot_general(
        mine, facing, (((1,), (0,)), ((), ())), precision=lax.Precision.HIGH, preferred_element_type=jnp.float32
    )

    held = [(mine, z)]
    up, down = mine, mine
    for step in (1, 2, 3):
        up = shift(up, dz=1)
        down = shift(down, dz=-1)
        held.append((up, (z - step + NZ) % NZ))
        held.append((down, (z + step) % NZ))
    up = shift(up[:half], dz=1)
    down = shift(down[half:], dz=-1)
    held.append((jnp.concatenate([up, down]), (z + 4) % NZ))

    inv_row = jnp.zeros((2, width, cols), jnp.float32)

    def put(out, value, k, owner):
        return lax.dynamic_update_slice(out, value[None], (k, 0, owner * chunk))

    for value, owner in held:
        inv_row = put(inv_row, value, core, owner)
    for group in (held[:3], held[3:5], held[5:7], held[7:]):
        got = shift(jnp.stack([value for value, _ in group]), fc=1)
        for i, (_, owner) in enumerate(group):
            inv_row = put(inv_row, got[i], 1 - core, owner)

    for move in (dict(fx=1), dict(fx=2), dict(fyl=1), dict(fz=1), dict(fz=2), dict(fz=4)):
        diag = diag + shift(diag, **move)
    diag_other = shift(diag, fc=1)
    pair = jnp.where(core == 0, jnp.stack([diag, diag_other]), jnp.stack([diag_other, diag]))
    return inv_row, dinv - pair


def solution(mesh):
    in_specs = (P(), P(None, "prow", None), P("prow", "pcol"), P())
    out_specs = (P(None, None, "pcol"), P())
    return jax.shard_map(local, mesh=mesh, in_specs=in_specs, out_specs=out_specs, check_vma=False)
```

time: 672 us -> 176 us (0.26)
  waiting for transfers between devices: 621 us -> 66.9 us
  starting transfers between devices: 0.12 us -> 56.2 us
  local copies, waits for them, and re-layouts: 3.06 us -> 24.2 us
  matrix products: 21.1 us -> 0.34 us
  Pallas kernels: 0 us -> 18.5 us
  between operations: 13.8 us -> 1.17 us
    psum x3 -> x0, waiting for transfers between devices: 620 us -> none  [the longest x1 286 us: local(): summed = lax.psum(partial_value, 'prow')]
    ppermute x0 -> x31, waiting for transfers between devices: none -> 66.9 us  [the longest x30 66.9 us: shift(): return lax.ppermute(value, AXES, perm)]
    ppermute x0 -> x31, starting transfers between devices: none -> 56.2 us  [the longest x30 51.2 us: shift(): return lax.ppermute(value, AXES, perm)]
    dot_general x3 -> x1, matrix products: 21.1 us -> 0.34 us  [local(): lax.dot_general(mine, facing, (((1,), (0,)), ((), ())), precision=lax.Pre...]
    pallas_call x0 -> x4, Pallas kernels: none -> 18.5 us  [product(): pl.pallas_call(product_kernel, out_shape=jax.ShapeDtypeStruct((count, wid...]
    dynamic_update_slice x0 -> x14, local copies, waits for them, and re-layouts: none -> 10.3 us  [put(): return lax.dynamic_update_slice(out, value[None], (k, 0, owner * chunk))]
    unnamed x8 -> x11, local copies, waits for them, and re-layouts: 1.99 us -> 9.79 us
    another operation x2 -> x3, other arithmetic: 7.2 us -> 0.14 us  [local(): got = shift(jnp.stack([value for value, _ in group]), fc=1)]
  transfers between devices with their start and end apart: 3 -> 31, of which waited for: 3 -> 13; matrix products, arithmetic and copies ran while one was open for 1% -> 12% of each run, Pallas kernels for 0% -> 8%
where the time goes in v1:
time: 176 us
  waiting for transfers between devices  66.9 us (38%)
  starting transfers between devices  56.2 us (32%)
  local copies, waits for them, and re-layouts  24.2 us (14%)
  Pallas kernels  18.5 us (11%)
  other arithmetic  8.31 us (5%)
    ppermute x30, waiting for transfers between devices, shift(): return lax.ppermute(value, AXES, perm)  66.9 us
    ppermute x30, starting transfers between devices, shift(): return lax.ppermute(value, AXES, perm)  51.2 us
    pallas_call x4, Pallas kernels, product(): pl.pallas_call(product_kernel, out_shape=jax.ShapeDtypeStruct((count, wid...  18.5 us
    dynamic_update_slice x14, local copies, waits for them, and re-layouts, put(): return lax.dynamic_update_slice(out, value[None], (k, 0, owner * chunk))  10.3 us
    unnamed x11, local copies, waits for them, and re-layouts  9.79 us
    ppermute x1, starting transfers between devices, local(): facing = lax.ppermute(give, AXES, perm)  5.01 us
  transfers between devices with their start and end apart: 31, of which 13 were waited for; matrix products, arithmetic and copies ran while one was open for 12% of the time, Pallas kernels for 8%

profile of v1, /device:TPU:1, one launch (start us, length us, event | category | flops | bytes accessed | tf_op | source)
XLA Modules:
  0.0 175.6 jit_solution(4867809073339277799)
XLA Ops:
  0.8 1.7 copy.10.panel_ref
  2.7 3.7 %copy-done = f32[768,3072]{1,0:T(8,128)S(1)} copy-done((f32[768,3072]{1,0:T(8,128)S(1)}, f32[768,3072]{1,0:T(8,128)}, u32[]{:S(2)}) %copy-start) | copy-done | bytes 9437208
  7.0 4.3 %shard_map.62 = f32[3,192,384]{2,1,0:T(8,128)} custom-call(s32[10]{0:T(128)S(1)} %stack.91.meta, s32[2,80]{1,0:T(2,128)S(1)} %copy-done.2, f32[2,768,192]{2,1,0:T(8,128)S(1)} %copy.10.panel_ref, f32[768,3072]{1,0:T(8,128)S(1)} %copy-done), custom_call_target="tpu_custom_call" | custom-call | flops 1019215872 | bytes 3538944 | tf_op jit(solution)/shard_map/pallas_call | solution.py:71
  11.3 3.2 %collective-permute-start.1 = (f32[3,192,384]{2,1,0:T(8,128)}, f32[3,192,384]{2,1,0:T(8,128)}, u32[]{:S(2)}, u32[]{:S(2)}) collective-permute-start(f32[3,192,384]{2,1,0:T(8,128)} %shard_map.62), channel_id=1, source_target_pairs={{0,8},{1,9},{2,10},{3,11},{4,12},{5,13},{6,14},{7,15},{8,0},{9,1},... | collective-permute-start | bytes 2654216 | tf_op jit(solution)/shard_map/ppermute | solution.py:35
  14.5 5.7 %shard_map.60 = f32[5,192,384]{2,1,0:T(8,128)} custom-call(s32[10]{0:T(128)S(1)} %stack.91.meta, s32[2,80]{1,0:T(2,128)S(1)} %copy-done.2, f32[2,768,192]{2,1,0:T(8,128)S(1)} %copy.10.panel_ref, f32[768,3072]{1,0:T(8,128)S(1)} %copy-done), custom_call_target="tpu_custom_call" | custom-call | flops 1698693120 | bytes 5898240 | tf_op jit(solution)/shard_map/pallas_call | solution.py:71
  20.4 3.7 %copy-done.1 = f32[768,3072]{1,0:T(8,128)S(1)} copy-done((f32[768,3072]{1,0:T(8,128)S(1)}, f32[768,3072]{1,0:T(8,128)}, u32[]{:S(2)}) %copy-start.1) | copy-done | bytes 9437208
  24.0 3.5 %shard_map.61 = f32[3,192,384]{2,1,0:T(8,128)S(1)} custom-call(s32[10]{0:T(128)S(1)} %stack.89.meta, s32[2,80]{1,0:T(2,128)S(1)} %copy-done.3, f32[2,768,192]{2,1,0:T(8,128)S(1)} %copy.10.panel_ref, f32[768,3072]{1,0:T(8,128)S(1)} %copy-done.1), custom_call_target="tpu_custom_call" | custom-call | flops 1019215872 | bytes 3538944 | tf_op jit(solution)/shard_map/pallas_call | solution.py:71
  27.6 5.0 %shard_map.59 = f32[5,192,384]{2,1,0:T(8,128)S(1)} custom-call(s32[10]{0:T(128)S(1)} %stack.89.meta, s32[2,80]{1,0:T(2,128)S(1)} %copy-done.3, f32[2,768,192]{2,1,0:T(8,128)S(1)} %copy.10.panel_ref, f32[768,3072]{1,0:T(8,128)S(1)} %copy-done.1), custom_call_target="tpu_custom_call" | custom-call | flops 1698693120 | bytes 5898240 | tf_op jit(solution)/shard_map/pallas_call | solution.py:71
  34.0 3.9 %collective-permute-start.6 = (f32[96,384]{1,0:T(8,128)S(1)}, f32[96,384]{1,0:T(8,128)S(1)}, u32[]{:S(2)}, u32[]{:S(2)}) collective-permute-start(f32[96,384]{1,0:T(8,128)S(1)} %get-tuple-element.10), channel_id=1, source_target_pairs={{0,224},{1,225},{2,226},{3,227},{4,228},{5,229},{6,230},{7,231},{8... | collective-permute-start | bytes 442376 | tf_op jit(solution)/shard_map/ppermute | solution.py:35
  37.9 3.6 %collective-permute-done.2 = f32[96,384]{1,0:T(8,128)S(1)} collective-permute-done((f32[96,384]{1,0:T(8,128)S(1)}, f32[96,384]{1,0:T(8,128)S(1)}, u32[]{:S(2)}, u32[]{:S(2)}) %collective-permute-start.2) | collective-permute-done | bytes 147488 | tf_op jit(solution)/shard_map/ppermute | solution.py:35
  41.8 2.7 %collective-permute-start.7 = (f32[192,384]{1,0:T(8,128)S(1)}, f32[192,384]{1,0:T(8,128)S(1)}, u32[]{:S(2)}, u32[]{:S(2)}) collective-permute-start(f32[192,384]{1,0:T(8,128)S(1)} %pad_maximum_fusion.4), channel_id=1, source_target_pairs={{0,224},{1,225},{2,226},{3,227},{4,228},{5,229},{6,230},{7,231},{8... | collective-permute-start | bytes 884744 | tf_op jit(solution)/shard_map/ppermute | solution.py:35
  44.5 5.9 %collective-permute-done.3 = f32[192,384]{1,0:T(8,128)S(1)} collective-permute-done((f32[192,384]{1,0:T(8,128)S(1)}, f32[192,384]{1,0:T(8,128)S(1)}, u32[]{:S(2)}, u32[]{:S(2)}) %collective-permute-start.3) | collective-permute-done | bytes 294944 | tf_op jit(solution)/shard_map/ppermute | solution.py:35
  51.5 7.7 %collective-permute-done.4 = f32[192,384]{1,0:T(8,128)S(1)} collective-permute-done((f32[192,384]{1,0:T(8,128)S(1)}, f32[192,384]{1,0:T(8,128)S(1)}, u32[]{:S(2)}, u32[]{:S(2)}) %collective-permute-start.4) | collective-permute-done | bytes 294944 | tf_op jit(solution)/shard_map/ppermute | solution.py:35
  61.9 4.1 %collective-permute-done.8 = f32[192,384]{1,0:T(8,128)S(1)} collective-permute-done((f32[192,384]{1,0:T(8,128)S(1)}, f32[192,384]{1,0:T(8,128)S(1)}, u32[]{:S(2)}, u32[]{:S(2)}) %collective-permute-start.8) | collective-permute-done | bytes 294944 | tf_op jit(solution)/shard_map/ppermute | solution.py:35
  67.0 1.8 %collective-permute-start.9 = (f32[192,384]{1,0:T(8,128)S(1)}, f32[192,384]{1,0:T(8,128)S(1)}, u32[]{:S(2)}, u32[]{:S(2)}) collective-permute-start(f32[192,384]{1,0:T(8,128)S(1)} %fusion.4), channel_id=1, source_target_pairs={{0,224},{1,225},{2,226},{3,227},{4,228},{5,229},{6,230},{7,231},{8... | collective-permute-start | bytes 884744 | tf_op jit(solution)/shard_map/ppermute | solution.py:35
  69.8 5.0 %collective-permute-start.23 = (f32[384,192]{0,1:T(8,128)S(1)}, f32[384,192]{0,1:T(8,128)S(1)}, u32[]{:S(2)}, u32[]{:S(2)}) collective-permute-start(f32[384,192]{0,1:T(8,128)S(1)} %dynamic-slice_bitcast_fusion), channel_id=1, source_target_pairs={{0,0},{1,8},{2,16},{3,24},{4,32},{5,40},{6,48},{7,56},{8,64},{9,72... | collective-permute-start | bytes 884744 | tf_op jit(solution)/shard_map/ppermute | solution.py:116
  75.9 4.1 %collective-permute-start.10 = (f32[192,384]{1,0:T(8,128)S(1)}, f32[192,384]{1,0:T(8,128)S(1)}, u32[]{:S(2)}, u32[]{:S(2)}) collective-permute-start(f32[192,384]{1,0:T(8,128)S(1)} %fusion.11), channel_id=1, source_target_pairs={{0,16},{1,17},{2,18},{3,19},{4,20},{5,21},{6,22},{7,23},{8,24},{9,... | collective-permute-start | bytes 884744 | tf_op jit(solution)/shard_map/ppermute | solution.py:35
  80.3 16.9 %collective-permute-done.10 = f32[192,384]{1,0:T(8,128)S(1)} collective-permute-done((f32[192,384]{1,0:T(8,128)S(1)}, f32[192,384]{1,0:T(8,128)S(1)}, u32[]{:S(2)}, u32[]{:S(2)}) %collective-permute-start.10) | collective-permute-done | bytes 294944 | tf_op jit(solution)/shard_map/ppermute | solution.py:35
  97.2 2.8 %broadcast_in_dim.31 = f32[2,192,3072]{2,1,0:T(8,128)} broadcast(f32[]{:T(128)} %constant.127.clone.1), dimensions={} | broadcast | bytes 4718596 | tf_op jit(solution)/shard_map/broadcast_in_dim | solution.py:173
  100.8 2.7 %collective-permute-start.12 = (f32[192,384]{1,0:T(8,128)S(1)}, f32[192,384]{1,0:T(8,128)S(1)}, u32[]{:S(2)}, u32[]{:S(2)}) collective-permute-start(f32[192,384]{1,0:T(8,128)S(1)} %get-tuple-element.3), channel_id=1, source_target_pairs={{0,224},{1,225},{2,226},{3,227},{4,228},{5,229},{6,230},{7,231},{8... | collective-permute-start | bytes 884744 | tf_op jit(solution)/shard_map/ppermute | solution.py:35
  103.9 5.3 %collective-permute-done.24 = f32[192,192]{1,0:T(8,128)S(1)} collective-permute-done((f32[192,192]{1,0:T(8,128)S(1)}, f32[192,192]{1,0:T(8,128)S(1)}, u32[]{:S(2)}, u32[]{:S(2)}) %collective-permute-start.24) | collective-permute-done | bytes 147488 | tf_op jit(solution)/shard_map/ppermute | solution.py:35
  110.2 7.9 %collective-permute-start.19 = (f32[3,192,384]{2,1,0:T(8,128)S(1)}, f32[3,192,384]{2,1,0:T(8,128)S(1)}, u32[]{:S(2)}, u32[]{:S(2)}) collective-permute-start(f32[3,192,384]{2,1,0:T(8,128)S(1)} %pad_maximum_fusion), channel_id=1, source_target_pairs={{0,8},{1,9},{2,10},{3,11},{4,12},{5,13},{6,14},{7,15},{8,0},{9,1},... | collective-permute-start | bytes 2654216 | tf_op jit(solution)/shard_map/ppermute | solution.py:35
  118.1 2.7 %collective-permute-start.14 = (f32[192,384]{1,0:T(8,128)S(1)}, f32[192,384]{1,0:T(8,128)S(1)}, u32[]{:S(2)}, u32[]{:S(2)}) collective-permute-start(f32[192,384]{1,0:T(8,128)S(1)} %collective-permute-done.12), channel_id=1, source_target_pairs={{0,224},{1,225},{2,226},{3,227},{4,228},{5,229},{6,230},{7,231},{8... | collective-permute-start | bytes 884744 | tf_op jit(solution)/shard_map/ppermute | solution.py:35
  121.7 4.9 %collective-permute-done.26 = f32[192,192]{1,0:T(8,128)S(1)} collective-permute-done((f32[192,192]{1,0:T(8,128)S(1)}, f32[192,192]{1,0:T(8,128)S(1)}, u32[]{:S(2)}, u32[]{:S(2)}) %collective-permute-start.26) | collective-permute-done | bytes 147488 | tf_op jit(solution)/shard_map/ppermute | solution.py:35
  129.2 1.9 %collective-permute-done.27 = f32[192,192]{1,0:T(8,128)S(1)} collective-permute-done((f32[192,192]{1,0:T(8,128)S(1)}, f32[192,192]{1,0:T(8,128)S(1)}, u32[]{:S(2)}, u32[]{:S(2)}) %collective-permute-start.27) | collective-permute-done | bytes 147488 | tf_op jit(solution)/shard_map/ppermute | solution.py:35
  131.2 3.8 %collective-permute-start.28 = (f32[192,192]{1,0:T(8,128)S(1)}, f32[192,192]{1,0:T(8,128)S(1)}, u32[]{:S(2)}, u32[]{:S(2)}) collective-permute-start(f32[192,192]{1,0:T(8,128)S(1)} %add.343), channel_id=1, source_target_pairs={{0,64},{1,65},{2,66},{3,67},{4,68},{5,69},{6,70},{7,71},{8,72},{9,... | collective-permute-start | bytes 442376 | tf_op jit(solution)/shard_map/ppermute | solution.py:35
  136.0 1.7 collective-permute-start.16
  138.4 5.4 %collective-permute-done.28 = f32[192,192]{1,0:T(8,128)S(1)} collective-permute-done((f32[192,192]{1,0:T(8,128)S(1)}, f32[192,192]{1,0:T(8,128)S(1)}, u32[]{:S(2)}, u32[]{:S(2)}) %collective-permute-start.28) | collective-permute-done | bytes 147488 | tf_op jit(solution)/shard_map/ppermute | solution.py:35
  143.8 4.4 %collective-permute-start.29 = (f32[192,192]{1,0:T(8,128)S(1)}, f32[192,192]{1,0:T(8,128)S(1)}, u32[]{:S(2)}, u32[]{:S(2)}) collective-permute-start(f32[192,192]{1,0:T(8,128)S(1)} %add.344), channel_id=1, source_target_pairs={{0,128},{1,129},{2,130},{3,131},{4,132},{5,133},{6,134},{7,135},{8... | collective-permute-start | bytes 442376 | tf_op jit(solution)/shard_map/ppermute | solution.py:35
  149.0 7.3 %collective-permute-done.29 = f32[192,192]{1,0:T(8,128)S(1)} collective-permute-done((f32[192,192]{1,0:T(8,128)S(1)}, f32[192,192]{1,0:T(8,128)S(1)}, u32[]{:S(2)}, u32[]{:S(2)}) %collective-permute-start.29) | collective-permute-done | bytes 147488 | tf_op jit(solution)/shard_map/ppermute | solution.py:35
  156.3 3.3 %collective-permute-start.30 = (f32[192,192]{1,0:T(8,128)S(1)}, f32[192,192]{1,0:T(8,128)S(1)}, u32[]{:S(2)}, u32[]{:S(2)}) collective-permute-start(f32[192,192]{1,0:T(8,128)S(1)} %add.345), channel_id=1, source_target_pairs={{0,8},{1,9},{2,10},{3,11},{4,12},{5,13},{6,14},{7,15},{8,0},{9,1},... | collective-permute-start | bytes 442376 | tf_op jit(solution)/shard_map/ppermute | solution.py:35
  165.4 2.3 %collective-permute-done.17 = f32[96,384]{1,0:T(8,128)S(1)} collective-permute-done((f32[96,384]{1,0:T(8,128)S(1)}, f32[96,384]{1,0:T(8,128)S(1)}, u32[]{:S(2)}, u32[]{:S(2)}) %collective-permute-start.17) | collective-permute-done | bytes 147488 | tf_op jit(solution)/shard_map/ppermute | solution.py:35
  (97 shorter events, 31.4 us)
Async XLA Ops:
  11.3 21.3 %collective-permute-start.1 = (f32[3,192,384]{2,1,0:T(8,128)}, f32[3,192,384]{2,1,0:T(8,128)}, u32[]{:S(2)}, u32[]{:S(2)}) collective-permute-start(f32[3,192,384]{2,1,0:T(8,128)} %shard_map.62), channel_id=1, source_target_pairs={{0,8},{1,9},{2,10},{3,11},{4,12},{5,13},{6,14},{7,15},{8,0},{9,1},... | collective-permute-start | bytes 2654216 | tf_op jit(solution)/shard_map/ppermute | solution.py:35
  20.3 30.1 %collective-permute-start = (f32[5,192,384]{2,1,0:T(8,128)}, f32[5,192,384]{2,1,0:T(8,128)}, u32[]{:S(2)}, u32[]{:S(2)}) collective-permute-start(f32[5,192,384]{2,1,0:T(8,128)} %shard_map.60), channel_id=1, source_target_pairs={{0,8},{1,9},{2,10},{3,11},{4,12},{5,13},{6,14},{7,15},{8,0},{9,1},... | collective-permute-start | bytes 4423688 | tf_op jit(solution)/shard_map/ppermute | solution.py:35
  33.9 7.7 %collective-permute-start.2 = (f32[96,384]{1,0:T(8,128)S(1)}, f32[96,384]{1,0:T(8,128)S(1)}, u32[]{:S(2)}, u32[]{:S(2)}) collective-permute-start(f32[96,384]{1,0:T(8,128)S(1)} %get-tuple-element.9), channel_id=1, source_target_pairs={{0,32},{1,33},{2,34},{3,35},{4,36},{5,37},{6,38},{7,39},{8,40},{9,... | collective-permute-start | bytes 442376 | tf_op jit(solution)/shard_map/ppermute | solution.py:35
  34.0 7.7 %collective-permute-start.6 = (f32[96,384]{1,0:T(8,128)S(1)}, f32[96,384]{1,0:T(8,128)S(1)}, u32[]{:S(2)}, u32[]{:S(2)}) collective-permute-start(f32[96,384]{1,0:T(8,128)S(1)} %get-tuple-element.10), channel_id=1, source_target_pairs={{0,224},{1,225},{2,226},{3,227},{4,228},{5,229},{6,230},{7,231},{8... | collective-permute-start | bytes 442376 | tf_op jit(solution)/shard_map/ppermute | solution.py:35
  41.6 8.8 %collective-permute-start.3 = (f32[192,384]{1,0:T(8,128)S(1)}, f32[192,384]{1,0:T(8,128)S(1)}, u32[]{:S(2)}, u32[]{:S(2)}) collective-permute-start(f32[192,384]{1,0:T(8,128)S(1)} %pad_maximum_fusion.3), channel_id=1, source_target_pairs={{0,32},{1,33},{2,34},{3,35},{4,36},{5,37},{6,38},{7,39},{8,40},{9,... | collective-permute-start | bytes 884744 | tf_op jit(solution)/shard_map/ppermute | solution.py:35
  41.8 9.7 %collective-permute-start.7 = (f32[192,384]{1,0:T(8,128)S(1)}, f32[192,384]{1,0:T(8,128)S(1)}, u32[]{:S(2)}, u32[]{:S(2)}) collective-permute-start(f32[192,384]{1,0:T(8,128)S(1)} %pad_maximum_fusion.4), channel_id=1, source_target_pairs={{0,224},{1,225},{2,226},{3,227},{4,228},{5,229},{6,230},{7,231},{8... | collective-permute-start | bytes 884744 | tf_op jit(solution)/shard_map/ppermute | solution.py:35
  51.4 7.8 %collective-permute-start.4 = (f32[192,384]{1,0:T(8,128)S(1)}, f32[192,384]{1,0:T(8,128)S(1)}, u32[]{:S(2)}, u32[]{:S(2)}) collective-permute-start(f32[192,384]{1,0:T(8,128)S(1)} %fusion.6), channel_id=1, source_target_pairs={{0,32},{1,33},{2,34},{3,35},{4,36},{5,37},{6,38},{7,39},{8,40},{9,... | collective-permute-start | bytes 884744 | tf_op jit(solution)/shard_map/ppermute | solution.py:35
  60.4 5.7 %collective-permute-start.8 = (f32[192,384]{1,0:T(8,128)S(1)}, f32[192,384]{1,0:T(8,128)S(1)}, u32[]{:S(2)}, u32[]{:S(2)}) collective-permute-start(f32[192,384]{1,0:T(8,128)S(1)} %get-tuple-element.5), channel_id=1, source_target_pairs={{0,224},{1,225},{2,226},{3,227},{4,228},{5,229},{6,230},{7,231},{8... | collective-permute-start | bytes 884744 | tf_op jit(solution)/shard_map/ppermute | solution.py:35
  60.4 14.4 %collective-permute-start.5 = (f32[192,384]{1,0:T(8,128)S(1)}, f32[192,384]{1,0:T(8,128)S(1)}, u32[]{:S(2)}, u32[]{:S(2)}) collective-permute-start(f32[192,384]{1,0:T(8,128)S(1)} %get-tuple-element.4), channel_id=1, source_target_pairs={{0,32},{1,33},{2,34},{3,35},{4,36},{5,37},{6,38},{7,39},{8,40},{9,... | collective-permute-start | bytes 884744 | tf_op jit(solution)/shard_map/ppermute | solution.py:35
  67.0 7.8 %collective-permute-start.9 = (f32[192,384]{1,0:T(8,128)S(1)}, f32[192,384]{1,0:T(8,128)S(1)}, u32[]{:S(2)}, u32[]{:S(2)}) collective-permute-start(f32[192,384]{1,0:T(8,128)S(1)} %fusion.4), channel_id=1, source_target_pairs={{0,224},{1,225},{2,226},{3,227},{4,228},{5,229},{6,230},{7,231},{8... | collective-permute-start | bytes 884744 | tf_op jit(solution)/shard_map/ppermute | solution.py:35
  69.8 33.6 %collective-permute-start.23 = (f32[384,192]{0,1:T(8,128)S(1)}, f32[384,192]{0,1:T(8,128)S(1)}, u32[]{:S(2)}, u32[]{:S(2)}) collective-permute-start(f32[384,192]{0,1:T(8,128)S(1)} %dynamic-slice_bitcast_fusion), channel_id=1, source_target_pairs={{0,0},{1,8},{2,16},{3,24},{4,32},{5,40},{6,48},{7,56},{8,64},{9,72... | collective-permute-start | bytes 884744 | tf_op jit(solution)/shard_map/ppermute | solution.py:116
  75.9 21.4 %collective-permute-start.10 = (f32[192,384]{1,0:T(8,128)S(1)}, f32[192,384]{1,0:T(8,128)S(1)}, u32[]{:S(2)}, u32[]{:S(2)}) collective-permute-start(f32[192,384]{1,0:T(8,128)S(1)} %fusion.11), channel_id=1, source_target_pairs={{0,16},{1,17},{2,18},{3,19},{4,20},{5,21},{6,22},{7,23},{8,24},{9,... | collective-permute-start | bytes 884744 | tf_op jit(solution)/shard_map/ppermute | solution.py:35
  100.7 9.4 %collective-permute-start.11 = (f32[192,384]{1,0:T(8,128)S(1)}, f32[192,384]{1,0:T(8,128)S(1)}, u32[]{:S(2)}, u32[]{:S(2)}) collective-permute-start(f32[192,384]{1,0:T(8,128)S(1)} %get-tuple-element.3), channel_id=1, source_target_pairs={{0,32},{1,33},{2,34},{3,35},{4,36},{5,37},{6,38},{7,39},{8,40},{9,... | collective-permute-start | bytes 884744 | tf_op jit(solution)/shard_map/ppermute | solution.py:35
  100.8 9.4 %collective-permute-start.12 = (f32[192,384]{1,0:T(8,128)S(1)}, f32[192,384]{1,0:T(8,128)S(1)}, u32[]{:S(2)}, u32[]{:S(2)}) collective-permute-start(f32[192,384]{1,0:T(8,128)S(1)} %get-tuple-element.3), channel_id=1, source_target_pairs={{0,224},{1,225},{2,226},{3,227},{4,228},{5,229},{6,230},{7,231},{8... | collective-permute-start | bytes 884744 | tf_op jit(solution)/shard_map/ppermute | solution.py:35
  103.8 5.4 %collective-permute-start.24 = (f32[192,192]{1,0:T(8,128)S(1)}, f32[192,192]{1,0:T(8,128)S(1)}, u32[]{:S(2)}, u32[]{:S(2)}) collective-permute-start(f32[192,192]{1,0:T(8,128)S(1)} %fusion.15), channel_id=1, source_target_pairs={{0,1},{1,0},{2,3},{3,2},{4,5},{5,4},{6,7},{7,6},{8,9},{9,8},{10,11... | collective-permute-start | bytes 442376 | tf_op jit(solution)/shard_map/ppermute | solution.py:35
  109.2 11.6 %collective-permute-start.25 = (f32[192,192]{1,0:T(8,128)S(1)}, f32[192,192]{1,0:T(8,128)S(1)}, u32[]{:S(2)}, u32[]{:S(2)}) collective-permute-start(f32[192,192]{1,0:T(8,128)S(1)} %add.340), channel_id=1, source_target_pairs={{0,2},{1,3},{2,0},{3,1},{4,6},{5,7},{6,4},{7,5},{8,10},{9,11},{10,... | collective-permute-start | bytes 442376 | tf_op jit(solution)/shard_map/ppermute | solution.py:35
  110.2 53.5 %copy-start.4 = (f32[2,192,192]{2,1,0:T(8,128)S(1)}, f32[2,192,192]{2,1,0:T(8,128)}, u32[]{:S(2)}) copy-start(f32[2,192,192]{2,1,0:T(8,128)} %param.7) | copy-start | bytes 884740
  110.2 59.5 %collective-permute-start.19 = (f32[3,192,384]{2,1,0:T(8,128)S(1)}, f32[3,192,384]{2,1,0:T(8,128)S(1)}, u32[]{:S(2)}, u32[]{:S(2)}) collective-permute-start(f32[3,192,384]{2,1,0:T(8,128)S(1)} %pad_maximum_fusion), channel_id=1, source_target_pairs={{0,8},{1,9},{2,10},{3,11},{4,12},{5,13},{6,14},{7,15},{8,0},{9,1},... | collective-permute-start | bytes 2654216 | tf_op jit(solution)/shard_map/ppermute | solution.py:35
  118.1 9.8 %collective-permute-start.13 = (f32[192,384]{1,0:T(8,128)S(1)}, f32[192,384]{1,0:T(8,128)S(1)}, u32[]{:S(2)}, u32[]{:S(2)}) collective-permute-start(f32[192,384]{1,0:T(8,128)S(1)} %collective-permute-done.11), channel_id=1, source_target_pairs={{0,32},{1,33},{2,34},{3,35},{4,36},{5,37},{6,38},{7,39},{8,40},{9,... | collective-permute-start | bytes 884744 | tf_op jit(solution)/shard_map/ppermute | solution.py:35
  118.1 9.8 %collective-permute-start.14 = (f32[192,384]{1,0:T(8,128)S(1)}, f32[192,384]{1,0:T(8,128)S(1)}, u32[]{:S(2)}, u32[]{:S(2)}) collective-permute-start(f32[192,384]{1,0:T(8,128)S(1)} %collective-permute-done.12), channel_id=1, source_target_pairs={{0,224},{1,225},{2,226},{3,227},{4,228},{5,229},{6,230},{7,231},{8... | collective-permute-start | bytes 884744 | tf_op jit(solution)/shard_map/ppermute | solution.py:35
  120.8 5.7 %collective-permute-start.26 = (f32[192,192]{1,0:T(8,128)S(1)}, f32[192,192]{1,0:T(8,128)S(1)}, u32[]{:S(2)}, u32[]{:S(2)}) collective-permute-start(f32[192,192]{1,0:T(8,128)S(1)} %add.341), channel_id=1, source_target_pairs={{0,4},{1,5},{2,6},{3,7},{4,0},{5,1},{6,2},{7,3},{8,12},{9,13},{10,... | collective-permute-start | bytes 442376 | tf_op jit(solution)/shard_map/ppermute | solution.py:35
  126.6 4.6 %collective-permute-start.27 = (f32[192,192]{1,0:T(8,128)S(1)}, f32[192,192]{1,0:T(8,128)S(1)}, u32[]{:S(2)}, u32[]{:S(2)}) collective-permute-start(f32[192,192]{1,0:T(8,128)S(1)} %add.342), channel_id=1, source_target_pairs={{0,32},{1,33},{2,34},{3,35},{4,36},{5,37},{6,38},{7,39},{8,40},{9,... | collective-permute-start | bytes 442376 | tf_op jit(solution)/shard_map/ppermute | solution.py:35
  127.9 44.0 %collective-permute-start.20 = (f32[2,192,384]{2,1,0:T(8,128)S(1)}, f32[2,192,384]{2,1,0:T(8,128)S(1)}, u32[]{:S(2)}, u32[]{:S(2)}) collective-permute-start(f32[2,192,384]{2,1,0:T(8,128)S(1)} %pad_maximum_fusion.1), channel_id=1, source_target_pairs={{0,8},{1,9},{2,10},{3,11},{4,12},{5,13},{6,14},{7,15},{8,0},{9,1},... | collective-permute-start | bytes 1769480 | tf_op jit(solution)/shard_map/ppermute | solution.py:35
  131.2 12.6 %collective-permute-start.28 = (f32[192,192]{1,0:T(8,128)S(1)}, f32[192,192]{1,0:T(8,128)S(1)}, u32[]{:S(2)}, u32[]{:S(2)}) collective-permute-start(f32[192,192]{1,0:T(8,128)S(1)} %add.343), channel_id=1, source_target_pairs={{0,64},{1,65},{2,66},{3,67},{4,68},{5,69},{6,70},{7,71},{8,72},{9,... | collective-permute-start | bytes 442376 | tf_op jit(solution)/shard_map/ppermute | solution.py:35
  135.0 26.3 %collective-permute-start.15 = (f32[192,384]{1,0:T(8,128)S(1)}, f32[192,384]{1,0:T(8,128)S(1)}, u32[]{:S(2)}, u32[]{:S(2)}) collective-permute-start(f32[192,384]{1,0:T(8,128)S(1)} %collective-permute-done.13), channel_id=1, source_target_pairs={{0,32},{1,33},{2,34},{3,35},{4,36},{5,37},{6,38},{7,39},{8,40},{9,... | collective-permute-start | bytes 884744 | tf_op jit(solution)/shard_map/ppermute | solution.py:35
  136.0 23.6 %collective-permute-start.16 = (f32[192,384]{1,0:T(8,128)S(1)}, f32[192,384]{1,0:T(8,128)S(1)}, u32[]{:S(2)}, u32[]{:S(2)}) collective-permute-start(f32[192,384]{1,0:T(8,128)S(1)} %collective-permute-done.14), channel_id=1, source_target_pairs={{0,224},{1,225},{2,226},{3,227},{4,228},{5,229},{6,230},{7,231},{8... | collective-permute-start | bytes 884744 | tf_op jit(solution)/shard_map/ppermute | solution.py:35
  143.8 12.5 %collective-permute-start.29 = (f32[192,192]{1,0:T(8,128)S(1)}, f32[192,192]{1,0:T(8,128)S(1)}, u32[]{:S(2)}, u32[]{:S(2)}) collective-permute-start(f32[192,192]{1,0:T(8,128)S(1)} %add.344), channel_id=1, source_target_pairs={{0,128},{1,129},{2,130},{3,131},{4,132},{5,133},{6,134},{7,135},{8... | collective-permute-start | bytes 442376 | tf_op jit(solution)/shard_map/ppermute | solution.py:35
  156.3 6.7 %collective-permute-start.30 = (f32[192,192]{1,0:T(8,128)S(1)}, f32[192,192]{1,0:T(8,128)S(1)}, u32[]{:S(2)}, u32[]{:S(2)}) collective-permute-start(f32[192,192]{1,0:T(8,128)S(1)} %add.345), channel_id=1, source_target_pairs={{0,8},{1,9},{2,10},{3,11},{4,12},{5,13},{6,14},{7,15},{8,0},{9,1},... | collective-permute-start | bytes 442376 | tf_op jit(solution)/shard_map/ppermute | solution.py:35
  159.6 5.8 %collective-permute-start.18 = (f32[96,384]{1,0:T(8,128)S(1)}, f32[96,384]{1,0:T(8,128)S(1)}, u32[]{:S(2)}, u32[]{:S(2)}) collective-permute-start(f32[96,384]{1,0:T(8,128)S(1)} %slice.171), channel_id=1, source_target_pairs={{0,224},{1,225},{2,226},{3,227},{4,228},{5,229},{6,230},{7,231},{8... | collective-permute-start | bytes 442376 | tf_op jit(solution)/shard_map/ppermute | solution.py:35
  161.3 6.4 %collective-permute-start.17 = (f32[96,384]{1,0:T(8,128)S(1)}, f32[96,384]{1,0:T(8,128)S(1)}, u32[]{:S(2)}, u32[]{:S(2)}) collective-permute-start(f32[96,384]{1,0:T(8,128)S(1)} %slice.170), channel_id=1, source_target_pairs={{0,32},{1,33},{2,34},{3,35},{4,36},{5,37},{6,38},{7,39},{8,40},{9,... | collective-permute-start | bytes 442376 | tf_op jit(solution)/shard_map/ppermute | solution.py:35
  163.0 10.4 %collective-permute-start.21 = (f32[2,192,384]{2,1,0:T(8,128)S(1)}, f32[2,192,384]{2,1,0:T(8,128)S(1)}, u32[]{:S(2)}, u32[]{:S(2)}) collective-permute-start(f32[2,192,384]{2,1,0:T(8,128)S(1)} %pad_maximum_fusion.2), channel_id=1, source_target_pairs={{0,8},{1,9},{2,10},{3,11},{4,12},{5,13},{6,14},{7,15},{8,0},{9,1},... | collective-permute-start | bytes 1769480 | tf_op jit(solution)/shard_map/ppermute | solution.py:35
  167.8 7.1 %collective-permute-start.22 = (f32[1,192,384]{2,1,0:T(8,128)S(1)}, f32[1,192,384]{2,1,0:T(8,128)S(1)}, u32[]{:S(2)}, u32[]{:S(2)}) collective-permute-start(f32[1,192,384]{2,1,0:T(8,128)S(1)} %maximum_bitcast_fusion), channel_id=1, source_target_pairs={{0,8},{1,9},{2,10},{3,11},{4,12},{5,13},{6,14},{7,15},{8,0},{9,1},... | collective-permute-start | bytes 884744 | tf_op jit(solution)/shard_map/ppermute | solution.py:35
  (4 other events, 17.1 us)

commit v2 on v0

v2 whole, which is shorter than its diff:
```python
import functools

import jax
import jax.numpy as jnp
from jax import lax
from jax.experimental import pallas as pl
from jax.experimental.pallas import tpu as pltpu
from jax.sharding import PartitionSpec as P

AXES = ("prow", "pcol")
NZ, NYH, NC, NYL, NX = 8, 2, 2, 2, 4
SMALL = pl.CostEstimate(flops=1000, bytes_accessed=1000, transcendentals=0)


def rank(z, yh, c, yl, x):
    return ((z * NYH + yh) * NC + c) * (NYL * NX) + yl * NX + x


def places():
    return [
        (z, yh, c, yl, x)
        for z in range(NZ)
        for yh in range(NYH)
        for c in range(NC)
        for yl in range(NYL)
        for x in range(NX)
    ]


def shift(value, dz=0, fz=0, fyh=0, fc=0, fyl=0, fx=0):
    perm = [
        (rank(z, yh, c, yl, x), rank(((z + dz) % NZ) ^ fz, yh ^ fyh, c ^ fc, yl ^ fyl, x ^ fx))
        for z, yh, c, yl, x in places()
    ]
    return lax.ppermute(value, AXES, perm)


def ring(value):
    perm = [
        (rank(z, yh, c, yl, x), rank((z + 1 - 2 * c) % NZ, yh, c, yl, x)) for z, yh, c, yl, x in places()
    ]
    return lax.ppermute(value, AXES, perm)


def after(value, *others):
    return lax.optimization_barrier((value, *others))[0]


def split(value):
    high = value.astype(jnp.bfloat16)
    low = (value - high.astype(jnp.float32)).astype(jnp.bfloat16)
    return high, low


def dot(a, b):
    return lax.dot_general(a, b, (((1,), (0,)), ((), ())), preferred_element_type=jnp.float32)


def left_kernel(struct_hbm, panel_hbm, *refs):
    left, struct_v, panel_v, sems = refs[-4:]
    width = panel_v.shape[1]
    row_index = lax.axis_index("prow")
    core = row_index % NC
    loads = [
        pltpu.make_async_copy(struct_hbm, struct_v, sems.at[0]),
        pltpu.make_async_copy(panel_hbm, panel_v, sems.at[1]),
    ]
    for copy in loads:
        copy.start()
    for copy in loads:
        copy.wait()
    row_blocks = panel_v.shape[2] // width
    for k in range(2):
        column = core if k == 0 else 1 - core
        listed = struct_v[pl.ds(column, 1), :]
        for i in range(row_blocks):
            hit = jnp.where(listed == row_index * row_blocks + i, -1.0, 0.0)
            sign = jnp.min(hit, axis=1, keepdims=True)
            span = slice(i * width, (i + 1) * width)
            high, low = split(panel_v[column, :, span] * sign)
            left[k * width : (k + 1) * width, span] = high
            left[(2 + k) * width : (3 + k) * width, span] = low


def left_side(struct_rows, panel):
    _, width, rows = panel.shape
    hbm, vmem = pl.BlockSpec(memory_space=pltpu.HBM), pl.BlockSpec(memory_space=pltpu.VMEM)
    return pl.pallas_call(
        left_kernel,
        out_shape=jax.ShapeDtypeStruct((4 * width, rows), jnp.bfloat16),
        in_specs=[hbm, hbm],
        out_specs=vmem,
        scratch_shapes=[
            pltpu.VMEM(struct_rows.shape, jnp.int32),
            pltpu.VMEM(panel.shape, jnp.float32),
            pltpu.SemaphoreType.DMA((2,)),
        ],
        compiler_params=pltpu.CompilerParams(vmem_limit_bytes=14 * 1024 * 1024),
        cost_estimate=SMALL,
    )(struct_rows, panel)


def product_kernel(chunks, own_keep, other_keep, own_send, other_send, left, ainv_ref, *refs):
    keep_ref, send_ref = refs[-2:]
    _, width, cols = keep_ref.shape
    row_index = lax.axis_index("prow")
    z = row_index // (NYH * NC)
    way = 1 - 2 * (row_index % NC)
    for j in range(0, len(chunks), 2):
        some = chunks[j : j + 2]
        blocks = []
        for rel in some:
            owner = lax.rem(z + way * rel + NZ, NZ)
            blocks.append(ainv_ref[:, pl.ds(pl.multiple_of(owner * cols, 128), cols)])
        high, low = split(jnp.concatenate(blocks, axis=1))
        both = dot(left[...], high)
        total = (both[2 * width :] + dot(left[: 2 * width], low)) + both[: 2 * width]
        for i, rel in enumerate(some):
            own, other = (total[k * width : (k + 1) * width, i * cols : (i + 1) * cols] for k in (0, 1))
            if rel in own_keep:
                keep_ref[own_keep[rel]] = own
            if rel in other_keep:
                keep_ref[other_keep[rel]] = other
            if rel in own_send:
                send_ref[own_send[rel]] = own
            if rel in other_send:
                send_ref[other_send[rel]] = other


def product(chunks, own_keep, other_keep, own_send, other_send, ainv, left, wait_for=()):
    rows = ainv.shape[0]
    cols = ainv.shape[1] // NZ
    width = left.shape[0] // 4
    vmem, some = pl.BlockSpec(memory_space=pltpu.VMEM), pl.BlockSpec(memory_space=pl.ANY)
    outs = [
        jax.ShapeDtypeStruct((len(own_keep) + len(other_keep), width, cols), jnp.float32),
        jax.ShapeDtypeStruct((len(own_send) + len(other_send), width, cols), jnp.float32),
    ]
    return pl.pallas_call(
        functools.partial(product_kernel, chunks, own_keep, other_keep, own_send, other_send),
        out_shape=outs,
        in_specs=[vmem, vmem] + [some] * len(wait_for),
        out_specs=[vmem] * len(outs),
        compiler_params=pltpu.CompilerParams(vmem_limit_bytes=14 * 1024 * 1024),
        cost_estimate=SMALL,
    )(left, ainv, *wait_for)


def add_kernel(a_ref, b_ref, out_ref):
    out_ref[...] = a_ref[...] + b_ref[...]


def add(a, b):
    vmem = pl.BlockSpec(memory_space=pltpu.VMEM)
    return pl.pallas_call(
        add_kernel,
        out_shape=jax.ShapeDtypeStruct(a.shape, a.dtype),
        in_specs=[vmem, vmem],
        out_specs=vmem,
        cost_estimate=pl.CostEstimate(flops=0, bytes_accessed=2 * 10**7, transcendentals=0),
    )(a, b)


def put_kernel(pieces, has_out, *refs):
    sources = refs[: len(pieces)]
    out_ref, sems = refs[len(pieces) + has_out], refs[len(pieces) + has_out + 1]
    row_index = lax.axis_index("prow")
    z = row_index // (NYH * NC)
    core = row_index % NC
    way = 1 - 2 * core
    copies = []
    for ref, rels in zip(sources, pieces):
        cols = ref.shape[-1]
        for i, (other, rel) in enumerate(rels):
            column = 1 - core if other else core
            owner = lax.rem(z + way * rel + NZ, NZ)
            place = pl.ds(pl.multiple_of(owner * cols, 128), cols)
            block = ref if len(rels) == 1 else ref.at[i]
            copies.append(
                pltpu.make_async_copy(block.at[: out_ref.shape[1]], out_ref.at[column, :, place], sems.at[len(copies)])
            )
    for copy in copies:
        copy.start()
    for copy in copies:
        copy.wait()


def put(shape, values, pieces, out=None):
    count = sum(len(rels) for rels in pieces)
    operands = list(values) + ([] if out is None else [out])
    return pl.pallas_call(
        functools.partial(put_kernel, pieces, out is not None),
        out_shape=jax.ShapeDtypeStruct(shape, jnp.float32),
        in_specs=[pl.BlockSpec(memory_space=pltpu.VMEM)] * len(values)
        + [pl.BlockSpec(memory_space=pltpu.HBM)] * (len(operands) - len(values)),
        out_specs=pl.BlockSpec(memory_space=pltpu.HBM),
        scratch_shapes=[pltpu.SemaphoreType.DMA((count,))],
        input_output_aliases={} if out is None else {len(values): 0},
        cost_estimate=pl.CostEstimate(flops=0, bytes_accessed=count * 600000, transcendentals=0),
    )(*operands)


def local(struct_rows, lpanel, ainv, dinv):
    row_index = lax.axis_index("prow")
    col_index = lax.axis_index("pcol")
    z = row_index // (NYH * NC)
    core = row_index % NC
    panel = jnp.swapaxes(lpanel, 1, 2)
    _, width, rows = panel.shape
    cols = ainv.shape[1]
    chunk = cols // NZ
    chunk_blocks = chunk // width

    perm = []
    for pz, pyh, pc, pyl, px in places():
        dest_z = (pyh * NC + pc) * 2 + pyl
        perm.append((rank(pz, pyh, pc, pyl, px), rank(dest_z, px >> 1, px & 1, pz // NX, pz % NX)))
    give = lax.dynamic_slice(panel, (col_index % 2, 0, col_index // NX * chunk), (1, width, chunk))[0]
    facing = lax.ppermute(give, AXES, perm)

    left = left_side(struct_rows, panel)
    keep1, send1 = product((4, -3), {4: 0}, {}, {-3: 0}, {4: 1, -3: 2}, ainv, left)
    keep2, send2 = product((3, -2, -1), {3: 0}, {3: 1}, {-2: 0, -1: 1}, {-2: 2, -1: 3}, ainv, left)
    keep3, send3 = product((2, 1, 0), {2: 0, 1: 1, 0: 2}, {2: 3, 1: 4}, {}, {0: 0}, ainv, left)
    got1 = shift(after(send1, facing, keep2, keep3), fc=1)
    got2 = shift(send2, fc=1)
    got3 = shift(send3, fc=1)

    own_part = {
        4: keep1[0] + got1[1],
        3: keep2[0] + got1[2],
        2: keep3[0] + got2[2],
        1: keep3[1] + got2[3],
        0: keep3[2] + got3[0],
    }
    other_part = {3: keep2[1] + got1[0], 2: keep3[3] + got2[0], 1: keep3[4] + got2[1]}

    own_part = {rel: lax.optimization_barrier(value) for rel, value in own_part.items()}
    other_part = {rel: lax.optimization_barrier(value) for rel, value in other_part.items()}

    own_flow = ring(own_part[4])
    other_flow = ring(other_part[3])
    own_flow = ring(own_part[3] + own_flow)
    other_flow = ring(other_part[2] + other_flow)
    own_flow = ring(own_part[2] + own_flow)
    other_flow = ring(other_part[1] + other_flow)
    own_flow = ring(own_part[1] + own_flow)
    other_flow = shift(other_flow, fc=1)

    ids = (col_index * NZ + z) * chunk_blocks + jnp.arange(chunk_blocks, dtype=jnp.int32)
    listed = lax.dynamic_slice_in_dim(struct_rows, core, 1, 0)
    inside = jnp.any(listed[0][:, None] == ids[None, :], axis=0)
    col_mask = jnp.repeat(inside.astype(jnp.float32), width)[None, :]
    plane = ((own_part[0] + other_flow) + own_flow) * col_mask
    mine = add(plane, shift(plane, fyh=1))

    diag = lax.dot_general(
        plane, facing, (((1,), (1,)), ((), ())), precision=lax.Precision.HIGH, preferred_element_type=jnp.float32
    )
    x = col_index % NX
    quarter = width // NX

    def rows_of(j):
        return lax.dynamic_slice_in_dim(diag, (x ^ j) * quarter, quarter, 0)

    diag = rows_of(0) + sum(shift(rows_of(j), fx=j) for j in (1, 2, 3))
    over_y = [shift(diag, fyl=1), shift(diag, fyh=1), shift(diag, fyl=1, fyh=1)]

    def here(far):
        return ((False, -far),), ((True, -far),)

    def there(far):
        return ((True, far), (False, far))

    shape = (2, width, cols)

    own1 = ring(mine)
    own1, over_y = lax.optimization_barrier((own1, over_y))
    diag = diag + sum(over_y)
    tail = jnp.concatenate([diag[: quarter // 2], diag[quarter // 2 :]], axis=1)
    theirs = shift(mine, fc=1)
    other1 = ring(theirs)
    own2 = ring(jnp.concatenate([own1, tail]))
    other2 = ring(jnp.concatenate([other1, shift(tail, fc=1)]))
    there1 = shift(jnp.stack([own1, other1]), fc=1)
    own3 = ring(own2)
    other3 = ring(other2)
    there2 = shift(jnp.stack([own2[:width], other2[:width]]), fc=1)
    inv_row = put(shape, [mine, theirs, own1, other1, there1], [*here(0), *here(1), there(1)])
    own3, inv_row = lax.optimization_barrier((own3, inv_row))
    own4 = ring(own3)
    there3 = shift(jnp.stack([own3[:width], other3[:width]]), fc=1)
    inv_row = put(shape, [own2, other2, own3, other3, there2], [*here(2), *here(3), there(2)], inv_row)
    own4, inv_row = lax.optimization_barrier((own4, inv_row))
    last = ring(jnp.concatenate([own4[width:], other3[width:]]))
    there4 = shift(own4[:width], fc=1)
    inv_row = put(shape, [there3, own4, there4], [there(3), ((False, -4),), ((True, 4),)], inv_row)
    rows = tail.shape[0]
    own_sum = (tail + own2[width:]) + (own3[width:] + own4[width:]) + last[:rows]
    other_sum = (other2[width:] + other3[width:]) + last[rows:]
    from_there = shift(jnp.concatenate([other_sum, own_sum]), fc=1)
    own_sum, other_sum = own_sum + from_there[:rows], other_sum + from_there[rows:]
    both = jnp.where(core == 0, jnp.stack([own_sum, other_sum]), jnp.stack([other_sum, own_sum]))
    both = jnp.concatenate([both[:, :, :width], both[:, :, width:]], axis=1)
    over_x = [shift(both, fx=j) for j in (1, 2, 3)]
    inv_row, over_x = lax.optimization_barrier((inv_row, over_x))
    blocks = [both] + over_x
    blocks = [jnp.where(x % 2 == 0, blocks[j], blocks[j ^ 1]) for j in range(4)]
    blocks = [jnp.where(x < 2, blocks[j], blocks[j ^ 2]) for j in range(4)]
    total = jnp.concatenate(blocks, axis=1)
    return inv_row, dinv - total


def solution(mesh):
    in_specs = (P(), P(None, "prow", None), P("prow", "pcol"), P())
    out_specs = (P(None, None, "pcol"), P())
    return jax.shard_map(local, mesh=mesh, in_specs=in_specs, out_specs=out_specs, check_vma=False)
```

time: 672 us -> 138 us (0.21)
  waiting for transfers between devices: 621 us -> 19.3 us
  starting transfers between devices: 0.12 us -> 84.5 us
  matrix products: 21.1 us -> 0.34 us
  Pallas kernels: 0 us -> 17.1 us
  between operations: 13.8 us -> 1.13 us
  other arithmetic: 12.5 us -> 2.78 us
  local copies, waits for them, and re-layouts: 3.06 us -> 12.6 us
    psum x3 -> x0, waiting for transfers between devices: 620 us -> none  [the longest x1 286 us: local(): summed = lax.psum(partial_value, 'prow')]
    ppermute x0 -> x37, starting transfers between devices: none -> 84.5 us  [the longest x15 43.5 us: ring(): return lax.ppermute(value, AXES, perm)]
    dot_general x3 -> x1, matrix products: 21.1 us -> 0.34 us  [local(): lax.dot_general(plane, facing, (((1,), (1,)), ((), ())), precision=lax.Pr...]
    ppermute x0 -> x37, waiting for transfers between devices: none -> 19.3 us  [the longest x21 10.2 us: shift(): return lax.ppermute(value, AXES, perm)]
    pallas_call x0 -> x8, Pallas kernels: none -> 17.1 us  [the longest x3 7.67 us: put(): pl.pallas_call(functools.partial(put_kernel, pieces, out is not None), ou...]
    unnamed x8 -> x38, local copies, waits for them, and re-layouts: 1.99 us -> 10.3 us
    another operation x2 -> x4, other arithmetic: 7.2 us -> 0.13 us  [the longest x1 0.04 us: local(): there2 = shift(jnp.stack([own2[:width], other2[:width]]), fc=1)]
  transfers between devices with their start and end apart: 3 -> 37, of which waited for: 3 -> 17; matrix products, arithmetic and copies ran while one was open for 1% -> 2% of each run, Pallas kernels for 0% -> 12%
where the time goes in v2:
time: 138 us
  starting transfers between devices  84.5 us (61%)
  waiting for transfers between devices  19.3 us (14%)
  Pallas kernels  17.1 us (12%)
  local copies, waits for them, and re-layouts  12.6 us (9%)
  other arithmetic  2.78 us (2%)
    ppermute x15, starting transfers between devices, ring(): return lax.ppermute(value, AXES, perm)  43.5 us
    ppermute x21, starting transfers between devices, shift(): return lax.ppermute(value, AXES, perm)  34.7 us
    unnamed x38, local copies, waits for them, and re-layouts  10.3 us
    ppermute x21, waiting for transfers between devices, shift(): return lax.ppermute(value, AXES, perm)  10.2 us
    ppermute x15, waiting for transfers between devices, ring(): return lax.ppermute(value, AXES, perm)  9.03 us
    pallas_call x3, Pallas kernels, put(): pl.pallas_call(functools.partial(put_kernel, pieces, out is not None), ou...  7.67 us
    pallas_call x3, Pallas kernels, product(): pl.pallas_call(functools.partial(product_kernel, chunks, own_keep, other_...  6.89 us
    ppermute x1, starting transfers between devices, local(): facing = lax.ppermute(give, AXES, perm)  6.29 us
  transfers between devices with their start and end apart: 37, of which 17 were waited for; matrix products, arithmetic and copies ran while one was open for 2% of the time, Pallas kernels for 12%

profile of v2, /device:TPU:1, one launch (start us, length us, event | category | flops | bytes accessed | tf_op | source)
XLA Modules:
  0.0 137.7 jit_solution(4241742121788387760)
XLA Ops:
  1.7 6.3 %collective-permute-start.2 = (f32[192,384]{1,0:T(8,128)S(1)}, f32[192,384]{1,0:T(8,128)S(1)}, u32[]{:S(2)}, u32[]{:S(2)}) collective-permute-start(f32[192,384]{1,0:T(8,128)S(1)} %dynamic-slice_bitcast_fusion), channel_id=1, source_target_pairs={{0,0},{1,8},{2,16},{3,24},{4,32},{5,40},{6,48},{7,56},{8,64},{9,72... | collective-permute-start | bytes 884744 | tf_op jit(solution)/shard_map/ppermute | solution.py:219
  10.6 3.7 %copy-done = f32[768,3072]{1,0:T(8,128)S(1)} copy-done((f32[768,3072]{1,0:T(8,128)S(1)}, f32[768,3072]{1,0:T(8,128)}, u32[]{:S(2)}) %copy-start) | copy-done | bytes 9437208
  14.3 2.6 %shard_map.61 = (f32[2,192,384]{2,1,0:T(8,128)S(1)}, f32[4,192,384]{2,1,0:T(8,128)S(1)}) custom-call(bf16[768,768]{1,0:T(8,128)(2,1)S(1)} %shard_map.59.left, f32[768,3072]{1,0:T(8,128)S(1)} %copy-done), custom_call_target="tpu_custom_call" | custom-call | flops 1000 | bytes 1000 | tf_op jit(solution)/shard_map/pallas_call | solution.py:139
  17.0 2.6 %shard_map.60 = (f32[5,192,384]{2,1,0:T(8,128)S(1)}, f32[1,192,384]{2,1,0:T(8,128)S(1)}) custom-call(bf16[768,768]{1,0:T(8,128)(2,1)S(1)} %shard_map.59.left, f32[768,3072]{1,0:T(8,128)S(1)} %copy-done), custom_call_target="tpu_custom_call" | custom-call | flops 1000 | bytes 1000 | tf_op jit(solution)/shard_map/pallas_call | solution.py:139
  19.6 1.7 %shard_map.62 = (f32[1,192,384]{2,1,0:T(8,128)S(1)}, f32[3,192,384]{2,1,0:T(8,128)S(1)}) custom-call(bf16[768,768]{1,0:T(8,128)(2,1)S(1)} %shard_map.59.left, f32[768,3072]{1,0:T(8,128)S(1)} %copy-done), custom_call_target="tpu_custom_call" | custom-call | flops 1000 | bytes 1000 | tf_op jit(solution)/shard_map/pallas_call | solution.py:139
  21.9 2.0 %collective-permute-done.3 = f32[3,192,384]{2,1,0:T(8,128)S(1)} collective-permute-done((f32[3,192,384]{2,1,0:T(8,128)S(1)}, f32[3,192,384]{2,1,0:T(8,128)S(1)}, u32[]{:S(2)}, u32[]{:S(2)}) %collective-permute-start.3) | collective-permute-done | bytes 884768 | tf_op jit(solution)/shard_map/ppermute | solution.py:35
  24.0 13.1 %collective-permute-start.8 = (f32[192,384]{1,0:T(8,128)S(1)}, f32[192,384]{1,0:T(8,128)S(1)}, u32[]{:S(2)}, u32[]{:S(2)}) collective-permute-start(f32[192,384]{1,0:T(8,128)S(1)} %get-tuple-element.47), channel_id=1, source_target_pairs={{0,32},{1,33},{2,34},{3,35},{4,36},{5,37},{6,38},{7,39},{8,232},{9... | collective-permute-start | bytes 884744 | tf_op jit(solution)/shard_map/ppermute | solution.py:42
  37.3 3.4 %collective-permute-done.8 = f32[192,384]{1,0:T(8,128)S(1)} collective-permute-done((f32[192,384]{1,0:T(8,128)S(1)}, f32[192,384]{1,0:T(8,128)S(1)}, u32[]{:S(2)}, u32[]{:S(2)}) %collective-permute-start.8) | collective-permute-done | bytes 294944 | tf_op jit(solution)/shard_map/ppermute | solution.py:42
  40.8 3.2 %collective-permute-start.9 = (f32[192,384]{1,0:T(8,128)S(1)}, f32[192,384]{1,0:T(8,128)S(1)}, u32[]{:S(2)}, u32[]{:S(2)}) collective-permute-start(f32[192,384]{1,0:T(8,128)S(1)} %add.185), channel_id=1, source_target_pairs={{0,32},{1,33},{2,34},{3,35},{4,36},{5,37},{6,38},{7,39},{8,232},{9... | collective-permute-start | bytes 884744 | tf_op jit(solution)/shard_map/ppermute | solution.py:42
  44.0 3.1 %collective-permute-start.5 = (f32[192,384]{1,0:T(8,128)S(1)}, f32[192,384]{1,0:T(8,128)S(1)}, u32[]{:S(2)}, u32[]{:S(2)}) collective-permute-start(f32[192,384]{1,0:T(8,128)S(1)} %add.174), channel_id=1, source_target_pairs={{0,32},{1,33},{2,34},{3,35},{4,36},{5,37},{6,38},{7,39},{8,232},{9... | collective-permute-start | bytes 884744 | tf_op jit(solution)/shard_map/ppermute | solution.py:42
  47.7 3.2 %collective-permute-start.10 = (f32[192,384]{1,0:T(8,128)S(1)}, f32[192,384]{1,0:T(8,128)S(1)}, u32[]{:S(2)}, u32[]{:S(2)}) collective-permute-start(f32[192,384]{1,0:T(8,128)S(1)} %add.186), channel_id=1, source_target_pairs={{0,32},{1,33},{2,34},{3,35},{4,36},{5,37},{6,38},{7,39},{8,232},{9... | collective-permute-start | bytes 884744 | tf_op jit(solution)/shard_map/ppermute | solution.py:42
  50.9 3.3 %collective-permute-start.6 = (f32[192,384]{1,0:T(8,128)S(1)}, f32[192,384]{1,0:T(8,128)S(1)}, u32[]{:S(2)}, u32[]{:S(2)}) collective-permute-start(f32[192,384]{1,0:T(8,128)S(1)} %add.175), channel_id=1, source_target_pairs={{0,32},{1,33},{2,34},{3,35},{4,36},{5,37},{6,38},{7,39},{8,232},{9... | collective-permute-start | bytes 884744 | tf_op jit(solution)/shard_map/ppermute | solution.py:42
  54.6 3.2 %collective-permute-start.11 = (f32[192,384]{1,0:T(8,128)S(1)}, f32[192,384]{1,0:T(8,128)S(1)}, u32[]{:S(2)}, u32[]{:S(2)}) collective-permute-start(f32[192,384]{1,0:T(8,128)S(1)} %add.187), channel_id=1, source_target_pairs={{0,32},{1,33},{2,34},{3,35},{4,36},{5,37},{6,38},{7,39},{8,232},{9... | collective-permute-start | bytes 884744 | tf_op jit(solution)/shard_map/ppermute | solution.py:42
  57.9 3.8 %collective-permute-start.7 = (f32[192,384]{1,0:T(8,128)S(1)}, f32[192,384]{1,0:T(8,128)S(1)}, u32[]{:S(2)}, u32[]{:S(2)}) collective-permute-start(f32[192,384]{1,0:T(8,128)S(1)} %collective-permute-done.6), channel_id=1, source_target_pairs={{0,8},{1,9},{2,10},{3,11},{4,12},{5,13},{6,14},{7,15},{8,0},{9,1},... | collective-permute-start | bytes 884744 | tf_op jit(solution)/shard_map/ppermute | solution.py:35
  62.9 5.7 %collective-permute-start.12 = (f32[192,384]{1,0:T(8,128)S(1)}, f32[192,384]{1,0:T(8,128)S(1)}, u32[]{:S(2)}, u32[]{:S(2)}) collective-permute-start(f32[192,384]{1,0:T(8,128)S(1)} %add_multiply_fusion.a_ref), channel_id=1, source_target_pairs={{0,16},{1,17},{2,18},{3,19},{4,20},{5,21},{6,22},{7,23},{8,24},{9,... | collective-permute-start | bytes 884744 | tf_op jit(solution)/shard_map/ppermute | solution.py:35
  70.3 2.6 %collective-permute-start.16 = (f32[48,192]{1,0:T(8,128)S(1)}, f32[48,192]{1,0:T(8,128)S(1)}, u32[]{:S(2)}, u32[]{:S(2)}) collective-permute-start(f32[48,192]{1,0:T(8,128)S(1)} %get-tuple-element.53), channel_id=1, source_target_pairs={{0,3},{1,2},{2,1},{3,0},{4,7},{5,6},{6,5},{7,4},{8,11},{9,10},{10,... | collective-permute-start | bytes 110600 | tf_op jit(solution)/shard_map/ppermute | solution.py:35
  73.6 1.8 %shard_map.63.refs_0_ = f32[192,384]{1,0:T(8,128)} custom-call(f32[192,384]{1,0:T(8,128)} %copy-done.6, f32[192,384]{1,0:T(8,128)} %copy-done.18), custom_call_target="tpu_custom_call" | custom-call | bytes 20000000 | tf_op jit(solution)/shard_map/pallas_call | solution.py:155
  75.4 3.2 %collective-permute-start.13 = (f32[192,384]{1,0:T(8,128)}, f32[192,384]{1,0:T(8,128)S(1)}, u32[]{:S(2)}, u32[]{:S(2)}) collective-permute-start(f32[192,384]{1,0:T(8,128)} %shard_map.63.refs_0_), channel_id=1, source_target_pairs={{0,32},{1,33},{2,34},{3,35},{4,36},{5,37},{6,38},{7,39},{8,232},{9... | collective-permute-start | bytes 884744 | tf_op jit(solution)/shard_map/ppermute | solution.py:42
  80.2 2.9 %collective-permute-start.18 = (f32[48,192]{1,0:T(8,128)S(1)}, f32[48,192]{1,0:T(8,128)S(1)}, u32[]{:S(2)}, u32[]{:S(2)}) collective-permute-start(f32[48,192]{1,0:T(8,128)S(1)} %add_add_fusion.1), channel_id=1, source_target_pairs={{0,16},{1,17},{2,18},{3,19},{4,20},{5,21},{6,22},{7,23},{8,24},{9,... | collective-permute-start | bytes 110600 | tf_op jit(solution)/shard_map/ppermute | solution.py:35
  84.0 1.9 %collective-permute-done.18 = f32[48,192]{1,0:T(8,128)S(1)} collective-permute-done((f32[48,192]{1,0:T(8,128)S(1)}, f32[48,192]{1,0:T(8,128)S(1)}, u32[]{:S(2)}, u32[]{:S(2)}) %collective-permute-start.18) | collective-permute-done | bytes 36896 | tf_op jit(solution)/shard_map/ppermute | solution.py:35
  85.9 1.6 %collective-permute-done.19 = f32[48,192]{1,0:T(8,128)S(1)} collective-permute-done((f32[48,192]{1,0:T(8,128)S(1)}, f32[48,192]{1,0:T(8,128)S(1)}, u32[]{:S(2)}, u32[]{:S(2)}) %collective-permute-start.19) | collective-permute-done | bytes 36896 | tf_op jit(solution)/shard_map/ppermute | solution.py:35
  87.5 2.7 %collective-permute-start.23 = (f32[192,384]{1,0:T(8,128)S(1)}, f32[192,384]{1,0:T(8,128)S(1)}, u32[]{:S(2)}, u32[]{:S(2)}) collective-permute-start(f32[192,384]{1,0:T(8,128)S(1)} %collective-permute-done.22.refs_1_), channel_id=1, source_target_pairs={{0,32},{1,33},{2,34},{3,35},{4,36},{5,37},{6,38},{7,39},{8,232},{9... | collective-permute-start | bytes 884744 | tf_op jit(solution)/shard_map/ppermute | solution.py:42
  94.0 3.2 %collective-permute-start.26 = (f32[216,384]{1,0:T(8,128)S(1)}, f32[216,384]{1,0:T(8,128)S(1)}, u32[]{:S(2)}, u32[]{:S(2)}) collective-permute-start(f32[216,384]{1,0:T(8,128)S(1)} %pad_maximum_fusion.3), channel_id=1, source_target_pairs={{0,32},{1,33},{2,34},{3,35},{4,36},{5,37},{6,38},{7,39},{8,232},{9... | collective-permute-start | bytes 995336 | tf_op jit(solution)/shard_map/ppermute | solution.py:42
  97.5 3.1 %collective-permute-start.21 = (f32[216,384]{1,0:T(8,128)S(1)}, f32[216,384]{1,0:T(8,128)S(1)}, u32[]{:S(2)}, u32[]{:S(2)}) collective-permute-start(f32[216,384]{1,0:T(8,128)S(1)} %collective-permute-done.20.refs_0_), channel_id=1, source_target_pairs={{0,32},{1,33},{2,34},{3,35},{4,36},{5,37},{6,38},{7,39},{8,232},{9... | collective-permute-start | bytes 995336 | tf_op jit(solution)/shard_map/ppermute | solution.py:42
  101.3 4.2 %collective-permute-start.30 = (f32[2,192,384]{2,1,0:T(8,128)S(1)}, f32[2,192,384]{2,1,0:T(8,128)S(1)}, u32[]{:S(2)}, u32[]{:S(2)}) collective-permute-start(f32[2,192,384]{2,1,0:T(8,128)S(1)} %pad_maximum_fusion.2), channel_id=1, source_target_pairs={{0,8},{1,9},{2,10},{3,11},{4,12},{5,13},{6,14},{7,15},{8,0},{9,1},... | collective-permute-start | bytes 1769480 | tf_op jit(solution)/shard_map/ppermute | solution.py:35
  106.8 2.7 %shard_map.64.refs_5_ = f32[2,192,3072]{2,1,0:T(8,128)} custom-call(f32[192,384]{1,0:T(8,128)} %shard_map.63.refs_0_, f32[192,384]{1,0:T(8,128)} %copy-done.16, f32[192,384]{1,0:T(8,128)} %copy-done.4, f32[192,384]{1,0:T(8,128)} %copy-done.5, f32[2,192,384]{2,1,0:T(8,128)} %copy-done.13), custom_call_target="tpu_custom_call" | custom-call | bytes 3600000 | tf_op jit(solution)/shard_map/pallas_call | solution.py:191
  109.7 2.1 %collective-permute-done.27.refs_3_ = f32[216,384]{1,0:T(8,128)S(1)} collective-permute-done((f32[216,384]{1,0:T(8,128)S(1)}, f32[216,384]{1,0:T(8,128)S(1)}, u32[]{:S(2)}, u32[]{:S(2)}) %collective-permute-start.27) | collective-permute-done | bytes 331808 | tf_op jit(solution)/shard_map/ppermute | solution.py:42
  113.3 2.7 %shard_map.65.refs_3_ = f32[2,192,3072]{2,1,0:T(8,128)} custom-call(f32[216,384]{1,0:T(8,128)} %copy-done.9, f32[216,384]{1,0:T(8,128)} %copy-done.10, f32[216,384]{1,0:T(8,128)} %copy-done.11, f32[216,384]{1,0:T(8,128)} %copy-done.8, f32[2,192,384]{2,1,0:T(8,128)} %copy-done.14, f32[2,192,3072]{2,1,0:T(8,128)} %shard_map.64.refs_5_), custom_call_target="tpu_custom_call", output_to_operand_aliasing={{}: (5, {})} | custom-call | bytes 3600000 | tf_op jit(solution)/shard_map/pallas_call | solution.py:191
  120.3 4.8 %collective-permute-start.33 = (f32[48,384]{1,0:T(8,128)S(1)}, f32[48,384]{1,0:T(8,128)S(1)}, u32[]{:S(2)}, u32[]{:S(2)}) collective-permute-start(f32[48,384]{1,0:T(8,128)S(1)} %pad_maximum_fusion.6), channel_id=1, source_target_pairs={{0,8},{1,9},{2,10},{3,11},{4,12},{5,13},{6,14},{7,15},{8,0},{9,1},... | collective-permute-start | bytes 221192 | tf_op jit(solution)/shard_map/ppermute | solution.py:35
  126.2 3.4 %collective-permute-start.35 = (f32[2,48,192]{2,1,0:T(8,128)S(1)}, f32[2,48,192]{2,1,0:T(8,128)S(1)}, u32[]{:S(2)}, u32[]{:S(2)}) collective-permute-start(f32[2,48,192]{2,1,0:T(8,128)S(1)} %pad_maximum_fusion.4), channel_id=1, source_target_pairs={{0,2},{1,3},{2,0},{3,1},{4,6},{5,7},{6,4},{7,5},{8,10},{9,11},{10,... | collective-permute-start | bytes 221192 | tf_op jit(solution)/shard_map/ppermute | solution.py:35
  131.6 2.3 %shard_map.66 = f32[2,192,3072]{2,1,0:T(8,128)} custom-call(f32[2,192,384]{2,1,0:T(8,128)} %copy-done.12, f32[216,384]{1,0:T(8,128)} %copy-done.7, f32[192,384]{1,0:T(8,128)} %copy-done.17, f32[2,192,3072]{2,1,0:T(8,128)} %shard_map.65.refs_3_), custom_call_target="tpu_custom_call", output_to_operand_aliasing={{}: (3, {})} | custom-call | bytes 2400000 | tf_op jit(solution)/shard_map/pallas_call | solution.py:191
  134.3 2.6 %collective-permute-done.36 = f32[2,48,192]{2,1,0:T(8,128)S(1)} collective-permute-done((f32[2,48,192]{2,1,0:T(8,128)S(1)}, f32[2,48,192]{2,1,0:T(8,128)S(1)}, u32[]{:S(2)}, u32[]{:S(2)}) %collective-permute-start.36) | collective-permute-done | bytes 73760 | tf_op jit(solution)/shard_map/ppermute | solution.py:35
  (130 shorter events, 28.3 us)
Async XLA Ops:
  1.7 19.6 %collective-permute-start.2 = (f32[192,384]{1,0:T(8,128)S(1)}, f32[192,384]{1,0:T(8,128)S(1)}, u32[]{:S(2)}, u32[]{:S(2)}) collective-permute-start(f32[192,384]{1,0:T(8,128)S(1)} %dynamic-slice_bitcast_fusion), channel_id=1, source_target_pairs={{0,0},{1,8},{2,16},{3,24},{4,32},{5,40},{6,48},{7,56},{8,64},{9,72... | collective-permute-start | bytes 884744 | tf_op jit(solution)/shard_map/ppermute | solution.py:219
  16.9 20.3 %collective-permute-start.1 = (f32[4,192,384]{2,1,0:T(8,128)S(1)}, f32[4,192,384]{2,1,0:T(8,128)S(1)}, u32[]{:S(2)}, u32[]{:S(2)}) collective-permute-start(f32[4,192,384]{2,1,0:T(8,128)S(1)} %get-tuple-element.23), channel_id=1, source_target_pairs={{0,8},{1,9},{2,10},{3,11},{4,12},{5,13},{6,14},{7,15},{8,0},{9,1},... | collective-permute-start | bytes 3538952 | tf_op jit(solution)/shard_map/ppermute | solution.py:35
  21.8 15.3 %collective-permute-start = (f32[1,192,384]{2,1,0:T(8,128)S(1)}, f32[1,192,384]{2,1,0:T(8,128)S(1)}, u32[]{:S(2)}, u32[]{:S(2)}) collective-permute-start(f32[1,192,384]{2,1,0:T(8,128)S(1)} %get-tuple-element.22), channel_id=1, source_target_pairs={{0,8},{1,9},{2,10},{3,11},{4,12},{5,13},{6,14},{7,15},{8,0},{9,1},... | collective-permute-start | bytes 884744 | tf_op jit(solution)/shard_map/ppermute | solution.py:35
  24.0 16.7 %collective-permute-start.8 = (f32[192,384]{1,0:T(8,128)S(1)}, f32[192,384]{1,0:T(8,128)S(1)}, u32[]{:S(2)}, u32[]{:S(2)}) collective-permute-start(f32[192,384]{1,0:T(8,128)S(1)} %get-tuple-element.47), channel_id=1, source_target_pairs={{0,32},{1,33},{2,34},{3,35},{4,36},{5,37},{6,38},{7,39},{8,232},{9... | collective-permute-start | bytes 884744 | tf_op jit(solution)/shard_map/ppermute | solution.py:42
  37.1 6.9 %collective-permute-start.4 = (f32[192,384]{1,0:T(8,128)S(1)}, f32[192,384]{1,0:T(8,128)S(1)}, u32[]{:S(2)}, u32[]{:S(2)}) collective-permute-start(f32[192,384]{1,0:T(8,128)S(1)} %get-tuple-element.44), channel_id=1, source_target_pairs={{0,32},{1,33},{2,34},{3,35},{4,36},{5,37},{6,38},{7,39},{8,232},{9... | collective-permute-start | bytes 884744 | tf_op jit(solution)/shard_map/ppermute | solution.py:42
  40.8 6.9 %collective-permute-start.9 = (f32[192,384]{1,0:T(8,128)S(1)}, f32[192,384]{1,0:T(8,128)S(1)}, u32[]{:S(2)}, u32[]{:S(2)}) collective-permute-start(f32[192,384]{1,0:T(8,128)S(1)} %add.185), channel_id=1, source_target_pairs={{0,32},{1,33},{2,34},{3,35},{4,36},{5,37},{6,38},{7,39},{8,232},{9... | collective-permute-start | bytes 884744 | tf_op jit(solution)/shard_map/ppermute | solution.py:42
  44.0 6.8 %collective-permute-start.5 = (f32[192,384]{1,0:T(8,128)S(1)}, f32[192,384]{1,0:T(8,128)S(1)}, u32[]{:S(2)}, u32[]{:S(2)}) collective-permute-start(f32[192,384]{1,0:T(8,128)S(1)} %add.174), channel_id=1, source_target_pairs={{0,32},{1,33},{2,34},{3,35},{4,36},{5,37},{6,38},{7,39},{8,232},{9... | collective-permute-start | bytes 884744 | tf_op jit(solution)/shard_map/ppermute | solution.py:42
  47.7 6.9 %collective-permute-start.10 = (f32[192,384]{1,0:T(8,128)S(1)}, f32[192,384]{1,0:T(8,128)S(1)}, u32[]{:S(2)}, u32[]{:S(2)}) collective-permute-start(f32[192,384]{1,0:T(8,128)S(1)} %add.186), channel_id=1, source_target_pairs={{0,32},{1,33},{2,34},{3,35},{4,36},{5,37},{6,38},{7,39},{8,232},{9... | collective-permute-start | bytes 884744 | tf_op jit(solution)/shard_map/ppermute | solution.py:42
  50.9 7.0 %collective-permute-start.6 = (f32[192,384]{1,0:T(8,128)S(1)}, f32[192,384]{1,0:T(8,128)S(1)}, u32[]{:S(2)}, u32[]{:S(2)}) collective-permute-start(f32[192,384]{1,0:T(8,128)S(1)} %add.175), channel_id=1, source_target_pairs={{0,32},{1,33},{2,34},{3,35},{4,36},{5,37},{6,38},{7,39},{8,232},{9... | collective-permute-start | bytes 884744 | tf_op jit(solution)/shard_map/ppermute | solution.py:42
  54.6 8.3 %collective-permute-start.11 = (f32[192,384]{1,0:T(8,128)S(1)}, f32[192,384]{1,0:T(8,128)S(1)}, u32[]{:S(2)}, u32[]{:S(2)}) collective-permute-start(f32[192,384]{1,0:T(8,128)S(1)} %add.187), channel_id=1, source_target_pairs={{0,32},{1,33},{2,34},{3,35},{4,36},{5,37},{6,38},{7,39},{8,232},{9... | collective-permute-start | bytes 884744 | tf_op jit(solution)/shard_map/ppermute | solution.py:42
  57.9 5.0 %collective-permute-start.7 = (f32[192,384]{1,0:T(8,128)S(1)}, f32[192,384]{1,0:T(8,128)S(1)}, u32[]{:S(2)}, u32[]{:S(2)}) collective-permute-start(f32[192,384]{1,0:T(8,128)S(1)} %collective-permute-done.6), channel_id=1, source_target_pairs={{0,8},{1,9},{2,10},{3,11},{4,12},{5,13},{6,14},{7,15},{8,0},{9,1},... | collective-permute-start | bytes 884744 | tf_op jit(solution)/shard_map/ppermute | solution.py:35
  62.9 10.0 %collective-permute-start.12 = (f32[192,384]{1,0:T(8,128)S(1)}, f32[192,384]{1,0:T(8,128)S(1)}, u32[]{:S(2)}, u32[]{:S(2)}) collective-permute-start(f32[192,384]{1,0:T(8,128)S(1)} %add_multiply_fusion.a_ref), channel_id=1, source_target_pairs={{0,16},{1,17},{2,18},{3,19},{4,20},{5,21},{6,22},{7,23},{8,24},{9,... | collective-permute-start | bytes 884744 | tf_op jit(solution)/shard_map/ppermute | solution.py:35
  69.0 11.1 %collective-permute-start.14 = (f32[48,192]{1,0:T(8,128)S(1)}, f32[48,192]{1,0:T(8,128)S(1)}, u32[]{:S(2)}, u32[]{:S(2)}) collective-permute-start(f32[48,192]{1,0:T(8,128)S(1)} %get-tuple-element.54), channel_id=1, source_target_pairs={{0,1},{1,0},{2,3},{3,2},{4,5},{5,4},{6,7},{7,6},{8,9},{9,8},{10,11... | collective-permute-start | bytes 110600 | tf_op jit(solution)/shard_map/ppermute | solution.py:35
  69.1 11.0 %collective-permute-start.15 = (f32[48,192]{1,0:T(8,128)S(1)}, f32[48,192]{1,0:T(8,128)S(1)}, u32[]{:S(2)}, u32[]{:S(2)}) collective-permute-start(f32[48,192]{1,0:T(8,128)S(1)} %get-tuple-element.52), channel_id=1, source_target_pairs={{0,2},{1,3},{2,0},{3,1},{4,6},{5,7},{6,4},{7,5},{8,10},{9,11},{10,... | collective-permute-start | bytes 110600 | tf_op jit(solution)/shard_map/ppermute | solution.py:35
  70.3 9.7 %collective-permute-start.16 = (f32[48,192]{1,0:T(8,128)S(1)}, f32[48,192]{1,0:T(8,128)S(1)}, u32[]{:S(2)}, u32[]{:S(2)}) collective-permute-start(f32[48,192]{1,0:T(8,128)S(1)} %get-tuple-element.53), channel_id=1, source_target_pairs={{0,3},{1,2},{2,1},{3,0},{4,7},{5,6},{6,5},{7,4},{8,11},{9,10},{10,... | collective-permute-start | bytes 110600 | tf_op jit(solution)/shard_map/ppermute | solution.py:35
  75.4 12.1 %collective-permute-start.13 = (f32[192,384]{1,0:T(8,128)}, f32[192,384]{1,0:T(8,128)S(1)}, u32[]{:S(2)}, u32[]{:S(2)}) collective-permute-start(f32[192,384]{1,0:T(8,128)} %shard_map.63.refs_0_), channel_id=1, source_target_pairs={{0,32},{1,33},{2,34},{3,35},{4,36},{5,37},{6,38},{7,39},{8,232},{9... | collective-permute-start | bytes 884744 | tf_op jit(solution)/shard_map/ppermute | solution.py:42
  78.6 8.9 %collective-permute-start.22 = (f32[192,384]{1,0:T(8,128)}, f32[192,384]{1,0:T(8,128)S(1)}, u32[]{:S(2)}, u32[]{:S(2)}) collective-permute-start(f32[192,384]{1,0:T(8,128)} %shard_map.63.refs_0_), channel_id=1, source_target_pairs={{0,8},{1,9},{2,10},{3,11},{4,12},{5,13},{6,14},{7,15},{8,0},{9,1},... | collective-permute-start | bytes 884744 | tf_op jit(solution)/shard_map/ppermute | solution.py:35
  80.2 5.7 %collective-permute-start.18 = (f32[48,192]{1,0:T(8,128)S(1)}, f32[48,192]{1,0:T(8,128)S(1)}, u32[]{:S(2)}, u32[]{:S(2)}) collective-permute-start(f32[48,192]{1,0:T(8,128)S(1)} %add_add_fusion.1), channel_id=1, source_target_pairs={{0,16},{1,17},{2,18},{3,19},{4,20},{5,21},{6,22},{7,23},{8,24},{9,... | collective-permute-start | bytes 110600 | tf_op jit(solution)/shard_map/ppermute | solution.py:35
  87.5 6.4 %collective-permute-start.23 = (f32[192,384]{1,0:T(8,128)S(1)}, f32[192,384]{1,0:T(8,128)S(1)}, u32[]{:S(2)}, u32[]{:S(2)}) collective-permute-start(f32[192,384]{1,0:T(8,128)S(1)} %collective-permute-done.22.refs_1_), channel_id=1, source_target_pairs={{0,32},{1,33},{2,34},{3,35},{4,36},{5,37},{6,38},{7,39},{8,232},{9... | collective-permute-start | bytes 884744 | tf_op jit(solution)/shard_map/ppermute | solution.py:42
  90.3 7.1 %collective-permute-start.20 = (f32[216,384]{1,0:T(8,128)S(1)}, f32[216,384]{1,0:T(8,128)S(1)}, u32[]{:S(2)}, u32[]{:S(2)}) collective-permute-start(f32[216,384]{1,0:T(8,128)S(1)} %maximum_maximum_fusion), channel_id=1, source_target_pairs={{0,32},{1,33},{2,34},{3,35},{4,36},{5,37},{6,38},{7,39},{8,232},{9... | collective-permute-start | bytes 995336 | tf_op jit(solution)/shard_map/ppermute | solution.py:42
  94.0 7.3 %collective-permute-start.26 = (f32[216,384]{1,0:T(8,128)S(1)}, f32[216,384]{1,0:T(8,128)S(1)}, u32[]{:S(2)}, u32[]{:S(2)}) collective-permute-start(f32[216,384]{1,0:T(8,128)S(1)} %pad_maximum_fusion.3), channel_id=1, source_target_pairs={{0,32},{1,33},{2,34},{3,35},{4,36},{5,37},{6,38},{7,39},{8,232},{9... | collective-permute-start | bytes 995336 | tf_op jit(solution)/shard_map/ppermute | solution.py:42
  97.2 8.8 %collective-permute-start.24 = (f32[2,192,384]{2,1,0:T(8,128)S(1)}, f32[2,192,384]{2,1,0:T(8,128)S(1)}, u32[]{:S(2)}, u32[]{:S(2)}) collective-permute-start(f32[2,192,384]{2,1,0:T(8,128)S(1)} %pad_maximum_fusion), channel_id=1, source_target_pairs={{0,8},{1,9},{2,10},{3,11},{4,12},{5,13},{6,14},{7,15},{8,0},{9,1},... | collective-permute-start | bytes 1769480 | tf_op jit(solution)/shard_map/ppermute | solution.py:35
  97.5 12.0 %collective-permute-start.21 = (f32[216,384]{1,0:T(8,128)S(1)}, f32[216,384]{1,0:T(8,128)S(1)}, u32[]{:S(2)}, u32[]{:S(2)}) collective-permute-start(f32[216,384]{1,0:T(8,128)S(1)} %collective-permute-done.20.refs_0_), channel_id=1, source_target_pairs={{0,32},{1,33},{2,34},{3,35},{4,36},{5,37},{6,38},{7,39},{8,232},{9... | collective-permute-start | bytes 995336 | tf_op jit(solution)/shard_map/ppermute | solution.py:42
  101.3 10.4 %collective-permute-start.30 = (f32[2,192,384]{2,1,0:T(8,128)S(1)}, f32[2,192,384]{2,1,0:T(8,128)S(1)}, u32[]{:S(2)}, u32[]{:S(2)}) collective-permute-start(f32[2,192,384]{2,1,0:T(8,128)S(1)} %pad_maximum_fusion.2), channel_id=1, source_target_pairs={{0,8},{1,9},{2,10},{3,11},{4,12},{5,13},{6,14},{7,15},{8,0},{9,1},... | collective-permute-start | bytes 1769480 | tf_op jit(solution)/shard_map/ppermute | solution.py:35
  105.5 6.3 %collective-permute-start.27 = (f32[216,384]{1,0:T(8,128)S(1)}, f32[216,384]{1,0:T(8,128)S(1)}, u32[]{:S(2)}, u32[]{:S(2)}) collective-permute-start(f32[216,384]{1,0:T(8,128)S(1)} %collective-permute-done.26.refs_1_), channel_id=1, source_target_pairs={{0,32},{1,33},{2,34},{3,35},{4,36},{5,37},{6,38},{7,39},{8,232},{9... | collective-permute-start | bytes 995336 | tf_op jit(solution)/shard_map/ppermute | solution.py:42
  109.5 6.5 %collective-permute-start.29 = (f32[216,384]{1,0:T(8,128)S(1)}, f32[216,384]{1,0:T(8,128)S(1)}, u32[]{:S(2)}, u32[]{:S(2)}) collective-permute-start(f32[216,384]{1,0:T(8,128)S(1)} %collective-permute-done.21.refs_2_), channel_id=1, source_target_pairs={{0,32},{1,33},{2,34},{3,35},{4,36},{5,37},{6,38},{7,39},{8,232},{9... | collective-permute-start | bytes 995336 | tf_op jit(solution)/shard_map/ppermute | solution.py:42
  120.3 5.7 %collective-permute-start.33 = (f32[48,384]{1,0:T(8,128)S(1)}, f32[48,384]{1,0:T(8,128)S(1)}, u32[]{:S(2)}, u32[]{:S(2)}) collective-permute-start(f32[48,384]{1,0:T(8,128)S(1)} %pad_maximum_fusion.6), channel_id=1, source_target_pairs={{0,8},{1,9},{2,10},{3,11},{4,12},{5,13},{6,14},{7,15},{8,0},{9,1},... | collective-permute-start | bytes 221192 | tf_op jit(solution)/shard_map/ppermute | solution.py:35
  125.1 5.0 %collective-permute-start.28 = (f32[2,192,384]{2,1,0:T(8,128)S(1)}, f32[2,192,384]{2,1,0:T(8,128)S(1)}, u32[]{:S(2)}, u32[]{:S(2)}) collective-permute-start(f32[2,192,384]{2,1,0:T(8,128)S(1)} %pad_maximum_fusion.1), channel_id=1, source_target_pairs={{0,8},{1,9},{2,10},{3,11},{4,12},{5,13},{6,14},{7,15},{8,0},{9,1},... | collective-permute-start | bytes 1769480 | tf_op jit(solution)/shard_map/ppermute | solution.py:35
  125.3 4.8 %collective-permute-start.31 = (f32[192,384]{1,0:T(8,128)S(1)}, f32[192,384]{1,0:T(8,128)S(1)}, u32[]{:S(2)}, u32[]{:S(2)}) collective-permute-start(f32[192,384]{1,0:T(8,128)S(1)} %slice.118), channel_id=1, source_target_pairs={{0,8},{1,9},{2,10},{3,11},{4,12},{5,13},{6,14},{7,15},{8,0},{9,1},... | collective-permute-start | bytes 884744 | tf_op jit(solution)/shard_map/ppermute | solution.py:35
  126.1 7.8 %collective-permute-start.34 = (f32[2,48,192]{2,1,0:T(8,128)S(1)}, f32[2,48,192]{2,1,0:T(8,128)S(1)}, u32[]{:S(2)}, u32[]{:S(2)}) collective-permute-start(f32[2,48,192]{2,1,0:T(8,128)S(1)} %pad_maximum_fusion.4), channel_id=1, source_target_pairs={{0,1},{1,0},{2,3},{3,2},{4,5},{5,4},{6,7},{7,6},{8,9},{9,8},{10,11... | collective-permute-start | bytes 221192 | tf_op jit(solution)/shard_map/ppermute | solution.py:35
  126.2 8.0 %collective-permute-start.35 = (f32[2,48,192]{2,1,0:T(8,128)S(1)}, f32[2,48,192]{2,1,0:T(8,128)S(1)}, u32[]{:S(2)}, u32[]{:S(2)}) collective-permute-start(f32[2,48,192]{2,1,0:T(8,128)S(1)} %pad_maximum_fusion.4), channel_id=1, source_target_pairs={{0,2},{1,3},{2,0},{3,1},{4,6},{5,7},{6,4},{7,5},{8,10},{9,11},{10,... | collective-permute-start | bytes 221192 | tf_op jit(solution)/shard_map/ppermute | solution.py:35
  129.6 7.2 %collective-permute-start.36 = (f32[2,48,192]{2,1,0:T(8,128)S(1)}, f32[2,48,192]{2,1,0:T(8,128)S(1)}, u32[]{:S(2)}, u32[]{:S(2)}) collective-permute-start(f32[2,48,192]{2,1,0:T(8,128)S(1)} %pad_maximum_fusion.4), channel_id=1, source_target_pairs={{0,3},{1,2},{2,1},{3,0},{4,7},{5,6},{6,5},{7,4},{8,11},{9,10},{10,... | collective-permute-start | bytes 221192 | tf_op jit(solution)/shard_map/ppermute | solution.py:35
  (24 other events, 116.6 us)

commit v3 on v2

--- a/solution.py
+++ b/solution.py
@@ -157,6 +157,8 @@
         out_shape=jax.ShapeDtypeStruct(a.shape, a.dtype),
         in_specs=[vmem, vmem],
         out_specs=vmem,
+        input_output_aliases={1: 0},
+        compiler_params=pltpu.CompilerParams(vmem_limit_bytes=4 * 1024 * 1024),
         cost_estimate=pl.CostEstimate(flops=0, bytes_accessed=2 * 10**7, transcendentals=0),
     )(a, b)
 
@@ -196,6 +198,7 @@
         out_specs=pl.BlockSpec(memory_space=pltpu.HBM),
         scratch_shapes=[pltpu.SemaphoreType.DMA((count,))],
         input_output_aliases={} if out is None else {len(values): 0},
+        compiler_params=pltpu.CompilerParams(vmem_limit_bytes=8 * 1024 * 1024),
         cost_estimate=pl.CostEstimate(flops=0, bytes_accessed=count * 600000, transcendentals=0),
     )(*operands)
 
@@ -293,7 +296,7 @@
     inv_row = put(shape, [own2, other2, own3, other3, there2], [*here(2), *here(3), there(2)], inv_row)
     own4, inv_row = lax.optimization_barrier((own4, inv_row))
     last = ring(jnp.concatenate([own4[width:], other3[width:]]))
-    there4 = shift(own4[:width], fc=1)
+    there4 = shift(own4, fc=1)
     inv_row = put(shape, [there3, own4, there4], [there(3), ((False, -4),), ((True, 4),)], inv_row)
     rows = tail.shape[0]
     own_sum = (tail + own2[width:]) + (own3[width:] + own4[width:]) + last[:rows]

time: 138 us -> 135 us (0.978)
  waiting for transfers between devices: 19.3 us -> 26.3 us
  Pallas kernels: 17.1 us -> 11.2 us
  local copies, waits for them, and re-layouts: 12.6 us -> 6.97 us
  starting transfers between devices: 84.5 us -> 86.7 us
    ppermute x15, waiting for transfers between devices: 9.03 us -> 14.4 us  [ring(): return lax.ppermute(value, AXES, perm)]
    unnamed x38 -> x10, local copies, waits for them, and re-layouts: 10.3 us -> 5.63 us
    pallas_call x3, Pallas kernels: 7.67 us -> 3.59 us  [put(): pl.pallas_call(functools.partial(put_kernel, pieces, out is not None), ou...]
    ppermute x21, starting transfers between devices: 34.7 us -> 37.9 us  [shift(): return lax.ppermute(value, AXES, perm)]
    pallas_call x1, Pallas kernels: 1.81 us -> 0.05 us  [add(): pl.pallas_call(add_kernel, out_shape=jax.ShapeDtypeStruct(a.shape, a.dtyp...]
    ppermute x21, waiting for transfers between devices: 10.2 us -> 11.9 us  [shift(): return lax.ppermute(value, AXES, perm)]
  transfers between devices with their start and end apart: 37 -> 37, of which waited for: 17 -> 16; matrix products, arithmetic and copies ran while one was open for 2% -> 1% of each run, Pallas kernels for 12% -> 8%
where the time goes in v3:
time: 135 us; the launch traced here: 134 us
  starting transfers between devices  86.7 us (64%)
  waiting for transfers between devices  26.3 us (19%)
  Pallas kernels  11.2 us (8%)
  local copies, waits for them, and re-layouts  6.97 us (5%)
  other arithmetic  1.93 us (1%)
    ppermute x15, starting transfers between devices, ring(): return lax.ppermute(value, AXES, perm)  42.5 us
    ppermute x21, starting transfers between devices, shift(): return lax.ppermute(value, AXES, perm)  37.9 us
    ppermute x15, waiting for transfers between devices, ring(): return lax.ppermute(value, AXES, perm)  14.4 us
    ppermute x21, waiting for transfers between devices, shift(): return lax.ppermute(value, AXES, perm)  11.9 us
    pallas_call x3, Pallas kernels, product(): pl.pallas_call(functools.partial(product_kernel, chunks, own_keep, other_...  6.84 us
    ppermute x1, starting transfers between devices, local(): facing = lax.ppermute(give, AXES, perm)  6.29 us
    unnamed x10, local copies, waits for them, and re-layouts  5.63 us
    pallas_call x3, Pallas kernels, put(): pl.pallas_call(functools.partial(put_kernel, pieces, out is not None), ou...  3.59 us
  transfers between devices with their start and end apart: 37, of which 16 were waited for; matrix products, arithmetic and copies ran while one was open for 1% of the time, Pallas kernels for 8%

profile of v3, /device:TPU:1, one launch (start us, length us, event | category | flops | bytes accessed | tf_op | source)
XLA Modules:
  0.0 134.4 jit_solution(954146798020530044)
XLA Ops:
  1.7 6.3 %collective-permute-start.2 = (f32[192,384]{1,0:T(8,128)S(1)}, f32[192,384]{1,0:T(8,128)S(1)}, u32[]{:S(2)}, u32[]{:S(2)}) collective-permute-start(f32[192,384]{1,0:T(8,128)S(1)} %dynamic-slice_bitcast_fusion), channel_id=1, source_target_pairs={{0,0},{1,8},{2,16},{3,24},{4,32},{5,40},{6,48},{7,56},{8,64},{9,72... | collective-permute-start | bytes 884744 | tf_op jit(solution)/shard_map/ppermute | solution.py:222
  10.6 3.7 %copy-done = f32[768,3072]{1,0:T(8,128)S(1)} copy-done((f32[768,3072]{1,0:T(8,128)S(1)}, f32[768,3072]{1,0:T(8,128)}, u32[]{:S(2)}) %copy-start) | copy-done | bytes 9437208
  14.3 2.6 %shard_map.61 = (f32[2,192,384]{2,1,0:T(8,128)S(1)}, f32[4,192,384]{2,1,0:T(8,128)S(1)}) custom-call(bf16[768,768]{1,0:T(8,128)(2,1)S(1)} %shard_map.59.left, f32[768,3072]{1,0:T(8,128)S(1)} %copy-done), custom_call_target="tpu_custom_call" | custom-call | flops 1000 | bytes 1000 | tf_op jit(solution)/shard_map/pallas_call | solution.py:139
  17.0 2.6 %shard_map.60 = (f32[5,192,384]{2,1,0:T(8,128)S(1)}, f32[1,192,384]{2,1,0:T(8,128)S(1)}) custom-call(bf16[768,768]{1,0:T(8,128)(2,1)S(1)} %shard_map.59.left, f32[768,3072]{1,0:T(8,128)S(1)} %copy-done), custom_call_target="tpu_custom_call" | custom-call | flops 1000 | bytes 1000 | tf_op jit(solution)/shard_map/pallas_call | solution.py:139
  19.6 1.6 %shard_map.62 = (f32[1,192,384]{2,1,0:T(8,128)S(1)}, f32[3,192,384]{2,1,0:T(8,128)S(1)}) custom-call(bf16[768,768]{1,0:T(8,128)(2,1)S(1)} %shard_map.59.left, f32[768,3072]{1,0:T(8,128)S(1)} %copy-done), custom_call_target="tpu_custom_call" | custom-call | flops 1000 | bytes 1000 | tf_op jit(solution)/shard_map/pallas_call | solution.py:139
  21.9 2.0 %collective-permute-done.3 = f32[3,192,384]{2,1,0:T(8,128)S(1)} collective-permute-done((f32[3,192,384]{2,1,0:T(8,128)S(1)}, f32[3,192,384]{2,1,0:T(8,128)S(1)}, u32[]{:S(2)}, u32[]{:S(2)}) %collective-permute-start.3) | collective-permute-done | bytes 884768 | tf_op jit(solution)/shard_map/ppermute | solution.py:35
  23.9 13.1 %collective-permute-start.8 = (f32[192,384]{1,0:T(8,128)S(1)}, f32[192,384]{1,0:T(8,128)S(1)}, u32[]{:S(2)}, u32[]{:S(2)}) collective-permute-start(f32[192,384]{1,0:T(8,128)S(1)} %get-tuple-element.47), channel_id=1, source_target_pairs={{0,32},{1,33},{2,34},{3,35},{4,36},{5,37},{6,38},{7,39},{8,232},{9... | collective-permute-start | bytes 884744 | tf_op jit(solution)/shard_map/ppermute | solution.py:42
  37.3 3.4 %collective-permute-done.8 = f32[192,384]{1,0:T(8,128)S(1)} collective-permute-done((f32[192,384]{1,0:T(8,128)S(1)}, f32[192,384]{1,0:T(8,128)S(1)}, u32[]{:S(2)}, u32[]{:S(2)}) %collective-permute-start.8) | collective-permute-done | bytes 294944 | tf_op jit(solution)/shard_map/ppermute | solution.py:42
  40.8 3.2 %collective-permute-start.9 = (f32[192,384]{1,0:T(8,128)S(1)}, f32[192,384]{1,0:T(8,128)S(1)}, u32[]{:S(2)}, u32[]{:S(2)}) collective-permute-start(f32[192,384]{1,0:T(8,128)S(1)} %add.185), channel_id=1, source_target_pairs={{0,32},{1,33},{2,34},{3,35},{4,36},{5,37},{6,38},{7,39},{8,232},{9... | collective-permute-start | bytes 884744 | tf_op jit(solution)/shard_map/ppermute | solution.py:42
  44.0 3.1 %collective-permute-start.5 = (f32[192,384]{1,0:T(8,128)S(1)}, f32[192,384]{1,0:T(8,128)S(1)}, u32[]{:S(2)}, u32[]{:S(2)}) collective-permute-start(f32[192,384]{1,0:T(8,128)S(1)} %add.174), channel_id=1, source_target_pairs={{0,32},{1,33},{2,34},{3,35},{4,36},{5,37},{6,38},{7,39},{8,232},{9... | collective-permute-start | bytes 884744 | tf_op jit(solution)/shard_map/ppermute | solution.py:42
  47.6 3.2 %collective-permute-start.10 = (f32[192,384]{1,0:T(8,128)S(1)}, f32[192,384]{1,0:T(8,128)S(1)}, u32[]{:S(2)}, u32[]{:S(2)}) collective-permute-start(f32[192,384]{1,0:T(8,128)S(1)} %add.186), channel_id=1, source_target_pairs={{0,32},{1,33},{2,34},{3,35},{4,36},{5,37},{6,38},{7,39},{8,232},{9... | collective-permute-start | bytes 884744 | tf_op jit(solution)/shard_map/ppermute | solution.py:42
  50.9 3.3 %collective-permute-start.6 = (f32[192,384]{1,0:T(8,128)S(1)}, f32[192,384]{1,0:T(8,128)S(1)}, u32[]{:S(2)}, u32[]{:S(2)}) collective-permute-start(f32[192,384]{1,0:T(8,128)S(1)} %add.175), channel_id=1, source_target_pairs={{0,32},{1,33},{2,34},{3,35},{4,36},{5,37},{6,38},{7,39},{8,232},{9... | collective-permute-start | bytes 884744 | tf_op jit(solution)/shard_map/ppermute | solution.py:42
  54.5 3.2 %collective-permute-start.11 = (f32[192,384]{1,0:T(8,128)S(1)}, f32[192,384]{1,0:T(8,128)S(1)}, u32[]{:S(2)}, u32[]{:S(2)}) collective-permute-start(f32[192,384]{1,0:T(8,128)S(1)} %add.187), channel_id=1, source_target_pairs={{0,32},{1,33},{2,34},{3,35},{4,36},{5,37},{6,38},{7,39},{8,232},{9... | collective-permute-start | bytes 884744 | tf_op jit(solution)/shard_map/ppermute | solution.py:42
  57.9 3.8 %collective-permute-start.7 = (f32[192,384]{1,0:T(8,128)S(1)}, f32[192,384]{1,0:T(8,128)S(1)}, u32[]{:S(2)}, u32[]{:S(2)}) collective-permute-start(f32[192,384]{1,0:T(8,128)S(1)} %collective-permute-done.6), channel_id=1, source_target_pairs={{0,8},{1,9},{2,10},{3,11},{4,12},{5,13},{6,14},{7,15},{8,0},{9,1},... | collective-permute-start | bytes 884744 | tf_op jit(solution)/shard_map/ppermute | solution.py:35
  62.9 5.7 %collective-permute-start.12 = (f32[192,384]{1,0:T(8,128)S(1)}, f32[192,384]{1,0:T(8,128)S(1)}, u32[]{:S(2)}, u32[]{:S(2)}) collective-permute-start(f32[192,384]{1,0:T(8,128)S(1)} %add_multiply_fusion.a_ref), channel_id=1, source_target_pairs={{0,16},{1,17},{2,18},{3,19},{4,20},{5,21},{6,22},{7,23},{8,24},{9,... | collective-permute-start | bytes 884744 | tf_op jit(solution)/shard_map/ppermute | solution.py:35
  70.3 2.6 %collective-permute-start.16 = (f32[48,192]{1,0:T(8,128)S(1)}, f32[48,192]{1,0:T(8,128)S(1)}, u32[]{:S(2)}, u32[]{:S(2)}) collective-permute-start(f32[48,192]{1,0:T(8,128)S(1)} %get-tuple-element.53), channel_id=1, source_target_pairs={{0,3},{1,2},{2,1},{3,0},{4,7},{5,6},{6,5},{7,4},{8,11},{9,10},{10,... | collective-permute-start | bytes 110600 | tf_op jit(solution)/shard_map/ppermute | solution.py:35
  72.9 3.2 %collective-permute-start.13 = (f32[192,384]{1,0:T(8,128)S(1)}, f32[192,384]{1,0:T(8,128)S(1)}, u32[]{:S(2)}, u32[]{:S(2)}) collective-permute-start(f32[192,384]{1,0:T(8,128)S(1)} %shard_map.63.refs_0_), channel_id=1, source_target_pairs={{0,32},{1,33},{2,34},{3,35},{4,36},{5,37},{6,38},{7,39},{8,232},{9... | collective-permute-start | bytes 884744 | tf_op jit(solution)/shard_map/ppermute | solution.py:42
  77.8 2.9 %collective-permute-start.18 = (f32[48,192]{1,0:T(8,128)S(1)}, f32[48,192]{1,0:T(8,128)S(1)}, u32[]{:S(2)}, u32[]{:S(2)}) collective-permute-start(f32[48,192]{1,0:T(8,128)S(1)} %add_add_fusion.1), channel_id=1, source_target_pairs={{0,16},{1,17},{2,18},{3,19},{4,20},{5,21},{6,22},{7,23},{8,24},{9,... | collective-permute-start | bytes 110600 | tf_op jit(solution)/shard_map/ppermute | solution.py:35
  82.6 2.8 %collective-permute-done.19 = f32[48,192]{1,0:T(8,128)S(1)} collective-permute-done((f32[48,192]{1,0:T(8,128)S(1)}, f32[48,192]{1,0:T(8,128)S(1)}, u32[]{:S(2)}, u32[]{:S(2)}) %collective-permute-start.19) | collective-permute-done | bytes 36896 | tf_op jit(solution)/shard_map/ppermute | solution.py:35
  85.5 2.4 %collective-permute-start.23 = (f32[192,384]{1,0:T(8,128)S(1)}, f32[192,384]{1,0:T(8,128)S(1)}, u32[]{:S(2)}, u32[]{:S(2)}) collective-permute-start(f32[192,384]{1,0:T(8,128)S(1)} %collective-permute-done.22.refs_1_), channel_id=1, source_target_pairs={{0,32},{1,33},{2,34},{3,35},{4,36},{5,37},{6,38},{7,39},{8,232},{9... | collective-permute-start | bytes 884744 | tf_op jit(solution)/shard_map/ppermute | solution.py:42
  91.5 3.2 %collective-permute-start.26 = (f32[216,384]{1,0:T(8,128)S(1)}, f32[216,384]{1,0:T(8,128)S(1)}, u32[]{:S(2)}, u32[]{:S(2)}) collective-permute-start(f32[216,384]{1,0:T(8,128)S(1)} %pad_maximum_fusion.3), channel_id=1, source_target_pairs={{0,32},{1,33},{2,34},{3,35},{4,36},{5,37},{6,38},{7,39},{8,232},{9... | collective-permute-start | bytes 995336 | tf_op jit(solution)/shard_map/ppermute | solution.py:42
  94.8 2.2 %collective-permute-start.24 = (f32[2,192,384]{2,1,0:T(8,128)S(1)}, f32[2,192,384]{2,1,0:T(8,128)S(1)}, u32[]{:S(2)}, u32[]{:S(2)}) collective-permute-start(f32[2,192,384]{2,1,0:T(8,128)S(1)} %pad_maximum_fusion), channel_id=1, source_target_pairs={{0,8},{1,9},{2,10},{3,11},{4,12},{5,13},{6,14},{7,15},{8,0},{9,1},... | collective-permute-start | bytes 1769480 | tf_op jit(solution)/shard_map/ppermute | solution.py:35
  96.9 2.9 %collective-permute-start.21 = (f32[216,384]{1,0:T(8,128)S(1)}, f32[216,384]{1,0:T(8,128)S(1)}, u32[]{:S(2)}, u32[]{:S(2)}) collective-permute-start(f32[216,384]{1,0:T(8,128)S(1)} %collective-permute-done.20.refs_0_), channel_id=1, source_target_pairs={{0,32},{1,33},{2,34},{3,35},{4,36},{5,37},{6,38},{7,39},{8,232},{9... | collective-permute-start | bytes 995336 | tf_op jit(solution)/shard_map/ppermute | solution.py:42
  100.0 5.3 %collective-permute-start.30 = (f32[2,192,384]{2,1,0:T(8,128)S(1)}, f32[2,192,384]{2,1,0:T(8,128)S(1)}, u32[]{:S(2)}, u32[]{:S(2)}) collective-permute-start(f32[2,192,384]{2,1,0:T(8,128)S(1)} %pad_maximum_fusion.2), channel_id=1, source_target_pairs={{0,8},{1,9},{2,10},{3,11},{4,12},{5,13},{6,14},{7,15},{8,0},{9,1},... | collective-permute-start | bytes 1769480 | tf_op jit(solution)/shard_map/ppermute | solution.py:35
  107.1 4.5 %collective-permute-done.27.refs_3_ = f32[216,384]{1,0:T(8,128)S(1)} collective-permute-done((f32[216,384]{1,0:T(8,128)S(1)}, f32[216,384]{1,0:T(8,128)S(1)}, u32[]{:S(2)}, u32[]{:S(2)}) %collective-permute-start.27) | collective-permute-done | bytes 331808 | tf_op jit(solution)/shard_map/ppermute | solution.py:42
  112.8 2.3 %collective-permute-done.29.refs_1_ = f32[216,384]{1,0:T(8,128)S(1)} collective-permute-done((f32[216,384]{1,0:T(8,128)S(1)}, f32[216,384]{1,0:T(8,128)S(1)}, u32[]{:S(2)}, u32[]{:S(2)}) %collective-permute-start.29) | collective-permute-done | bytes 331808 | tf_op jit(solution)/shard_map/ppermute | solution.py:42
  116.1 2.3 %collective-permute-done.32 = f32[48,384]{1,0:T(8,128)S(1)} collective-permute-done((f32[48,384]{1,0:T(8,128)S(1)}, f32[48,384]{1,0:T(8,128)S(1)}, u32[]{:S(2)}, u32[]{:S(2)}) %collective-permute-start.32) | collective-permute-done | bytes 73760 | tf_op jit(solution)/shard_map/ppermute | solution.py:42
  118.5 4.8 %collective-permute-start.33 = (f32[48,384]{1,0:T(8,128)S(1)}, f32[48,384]{1,0:T(8,128)S(1)}, u32[]{:S(2)}, u32[]{:S(2)}) collective-permute-start(f32[48,384]{1,0:T(8,128)S(1)} %pad_maximum_fusion.6), channel_id=1, source_target_pairs={{0,8},{1,9},{2,10},{3,11},{4,12},{5,13},{6,14},{7,15},{8,0},{9,1},... | collective-permute-start | bytes 221192 | tf_op jit(solution)/shard_map/ppermute | solution.py:35
  124.4 1.9 %collective-permute-start.35 = (f32[2,48,192]{2,1,0:T(8,128)S(1)}, f32[2,48,192]{2,1,0:T(8,128)S(1)}, u32[]{:S(2)}, u32[]{:S(2)}) collective-permute-start(f32[2,48,192]{2,1,0:T(8,128)S(1)} %pad_maximum_fusion.4), channel_id=1, source_target_pairs={{0,2},{1,3},{2,0},{3,1},{4,6},{5,7},{6,4},{7,5},{8,10},{9,11},{10,... | collective-permute-start | bytes 221192 | tf_op jit(solution)/shard_map/ppermute | solution.py:35
  126.3 1.9 %collective-permute-start.36 = (f32[2,48,192]{2,1,0:T(8,128)S(1)}, f32[2,48,192]{2,1,0:T(8,128)S(1)}, u32[]{:S(2)}, u32[]{:S(2)}) collective-permute-start(f32[2,48,192]{2,1,0:T(8,128)S(1)} %pad_maximum_fusion.4), channel_id=1, source_target_pairs={{0,3},{1,2},{2,1},{3,0},{4,7},{5,6},{6,5},{7,4},{8,11},{9,10},{10,... | collective-permute-start | bytes 221192 | tf_op jit(solution)/shard_map/ppermute | solution.py:35
  129.4 1.6 %collective-permute-done.35 = f32[2,48,192]{2,1,0:T(8,128)S(1)} collective-permute-done((f32[2,48,192]{2,1,0:T(8,128)S(1)}, f32[2,48,192]{2,1,0:T(8,128)S(1)}, u32[]{:S(2)}, u32[]{:S(2)}) %collective-permute-start.35) | collective-permute-done | bytes 73760 | tf_op jit(solution)/shard_map/ppermute | solution.py:35
  131.0 2.6 %collective-permute-done.36 = f32[2,48,192]{2,1,0:T(8,128)S(1)} collective-permute-done((f32[2,48,192]{2,1,0:T(8,128)S(1)}, f32[2,48,192]{2,1,0:T(8,128)S(1)}, u32[]{:S(2)}, u32[]{:S(2)}) %collective-permute-start.36) | collective-permute-done | bytes 73760 | tf_op jit(solution)/shard_map/ppermute | solution.py:35
  (101 shorter events, 23.4 us)
Async XLA Ops:
  1.7 19.6 %collective-permute-start.2 = (f32[192,384]{1,0:T(8,128)S(1)}, f32[192,384]{1,0:T(8,128)S(1)}, u32[]{:S(2)}, u32[]{:S(2)}) collective-permute-start(f32[192,384]{1,0:T(8,128)S(1)} %dynamic-slice_bitcast_fusion), channel_id=1, source_target_pairs={{0,0},{1,8},{2,16},{3,24},{4,32},{5,40},{6,48},{7,56},{8,64},{9,72... | collective-permute-start | bytes 884744 | tf_op jit(solution)/shard_map/ppermute | solution.py:222
  16.9 20.3 %collective-permute-start.1 = (f32[4,192,384]{2,1,0:T(8,128)S(1)}, f32[4,192,384]{2,1,0:T(8,128)S(1)}, u32[]{:S(2)}, u32[]{:S(2)}) collective-permute-start(f32[4,192,384]{2,1,0:T(8,128)S(1)} %get-tuple-element.23), channel_id=1, source_target_pairs={{0,8},{1,9},{2,10},{3,11},{4,12},{5,13},{6,14},{7,15},{8,0},{9,1},... | collective-permute-start | bytes 3538952 | tf_op jit(solution)/shard_map/ppermute | solution.py:35
  21.8 15.4 %collective-permute-start = (f32[1,192,384]{2,1,0:T(8,128)S(1)}, f32[1,192,384]{2,1,0:T(8,128)S(1)}, u32[]{:S(2)}, u32[]{:S(2)}) collective-permute-start(f32[1,192,384]{2,1,0:T(8,128)S(1)} %get-tuple-element.22), channel_id=1, source_target_pairs={{0,8},{1,9},{2,10},{3,11},{4,12},{5,13},{6,14},{7,15},{8,0},{9,1},... | collective-permute-start | bytes 884744 | tf_op jit(solution)/shard_map/ppermute | solution.py:35
  23.9 16.8 %collective-permute-start.8 = (f32[192,384]{1,0:T(8,128)S(1)}, f32[192,384]{1,0:T(8,128)S(1)}, u32[]{:S(2)}, u32[]{:S(2)}) collective-permute-start(f32[192,384]{1,0:T(8,128)S(1)} %get-tuple-element.47), channel_id=1, source_target_pairs={{0,32},{1,33},{2,34},{3,35},{4,36},{5,37},{6,38},{7,39},{8,232},{9... | collective-permute-start | bytes 884744 | tf_op jit(solution)/shard_map/ppermute | solution.py:42
  37.0 6.9 %collective-permute-start.4 = (f32[192,384]{1,0:T(8,128)S(1)}, f32[192,384]{1,0:T(8,128)S(1)}, u32[]{:S(2)}, u32[]{:S(2)}) collective-permute-start(f32[192,384]{1,0:T(8,128)S(1)} %get-tuple-element.44), channel_id=1, source_target_pairs={{0,32},{1,33},{2,34},{3,35},{4,36},{5,37},{6,38},{7,39},{8,232},{9... | collective-permute-start | bytes 884744 | tf_op jit(solution)/shard_map/ppermute | solution.py:42
  40.8 6.9 %collective-permute-start.9 = (f32[192,384]{1,0:T(8,128)S(1)}, f32[192,384]{1,0:T(8,128)S(1)}, u32[]{:S(2)}, u32[]{:S(2)}) collective-permute-start(f32[192,384]{1,0:T(8,128)S(1)} %add.185), channel_id=1, source_target_pairs={{0,32},{1,33},{2,34},{3,35},{4,36},{5,37},{6,38},{7,39},{8,232},{9... | collective-permute-start | bytes 884744 | tf_op jit(solution)/shard_map/ppermute | solution.py:42
  44.0 6.8 %collective-permute-start.5 = (f32[192,384]{1,0:T(8,128)S(1)}, f32[192,384]{1,0:T(8,128)S(1)}, u32[]{:S(2)}, u32[]{:S(2)}) collective-permute-start(f32[192,384]{1,0:T(8,128)S(1)} %add.174), channel_id=1, source_target_pairs={{0,32},{1,33},{2,34},{3,35},{4,36},{5,37},{6,38},{7,39},{8,232},{9... | collective-permute-start | bytes 884744 | tf_op jit(solution)/shard_map/ppermute | solution.py:42
  47.6 6.9 %collective-permute-start.10 = (f32[192,384]{1,0:T(8,128)S(1)}, f32[192,384]{1,0:T(8,128)S(1)}, u32[]{:S(2)}, u32[]{:S(2)}) collective-permute-start(f32[192,384]{1,0:T(8,128)S(1)} %add.186), channel_id=1, source_target_pairs={{0,32},{1,33},{2,34},{3,35},{4,36},{5,37},{6,38},{7,39},{8,232},{9... | collective-permute-start | bytes 884744 | tf_op jit(solution)/shard_map/ppermute | solution.py:42
  50.9 7.0 %collective-permute-start.6 = (f32[192,384]{1,0:T(8,128)S(1)}, f32[192,384]{1,0:T(8,128)S(1)}, u32[]{:S(2)}, u32[]{:S(2)}) collective-permute-start(f32[192,384]{1,0:T(8,128)S(1)} %add.175), channel_id=1, source_target_pairs={{0,32},{1,33},{2,34},{3,35},{4,36},{5,37},{6,38},{7,39},{8,232},{9... | collective-permute-start | bytes 884744 | tf_op jit(solution)/shard_map/ppermute | solution.py:42
  54.5 8.3 %collective-permute-start.11 = (f32[192,384]{1,0:T(8,128)S(1)}, f32[192,384]{1,0:T(8,128)S(1)}, u32[]{:S(2)}, u32[]{:S(2)}) collective-permute-start(f32[192,384]{1,0:T(8,128)S(1)} %add.187), channel_id=1, source_target_pairs={{0,32},{1,33},{2,34},{3,35},{4,36},{5,37},{6,38},{7,39},{8,232},{9... | collective-permute-start | bytes 884744 | tf_op jit(solution)/shard_map/ppermute | solution.py:42
  57.9 5.0 %collective-permute-start.7 = (f32[192,384]{1,0:T(8,128)S(1)}, f32[192,384]{1,0:T(8,128)S(1)}, u32[]{:S(2)}, u32[]{:S(2)}) collective-permute-start(f32[192,384]{1,0:T(8,128)S(1)} %collective-permute-done.6), channel_id=1, source_target_pairs={{0,8},{1,9},{2,10},{3,11},{4,12},{5,13},{6,14},{7,15},{8,0},{9,1},... | collective-permute-start | bytes 884744 | tf_op jit(solution)/shard_map/ppermute | solution.py:35
  62.9 10.0 %collective-permute-start.12 = (f32[192,384]{1,0:T(8,128)S(1)}, f32[192,384]{1,0:T(8,128)S(1)}, u32[]{:S(2)}, u32[]{:S(2)}) collective-permute-start(f32[192,384]{1,0:T(8,128)S(1)} %add_multiply_fusion.a_ref), channel_id=1, source_target_pairs={{0,16},{1,17},{2,18},{3,19},{4,20},{5,21},{6,22},{7,23},{8,24},{9,... | collective-permute-start | bytes 884744 | tf_op jit(solution)/shard_map/ppermute | solution.py:35
  68.9 8.8 %collective-permute-start.14 = (f32[48,192]{1,0:T(8,128)S(1)}, f32[48,192]{1,0:T(8,128)S(1)}, u32[]{:S(2)}, u32[]{:S(2)}) collective-permute-start(f32[48,192]{1,0:T(8,128)S(1)} %get-tuple-element.54), channel_id=1, source_target_pairs={{0,1},{1,0},{2,3},{3,2},{4,5},{5,4},{6,7},{7,6},{8,9},{9,8},{10,11... | collective-permute-start | bytes 110600 | tf_op jit(solution)/shard_map/ppermute | solution.py:35
  69.0 8.7 %collective-permute-start.15 = (f32[48,192]{1,0:T(8,128)S(1)}, f32[48,192]{1,0:T(8,128)S(1)}, u32[]{:S(2)}, u32[]{:S(2)}) collective-permute-start(f32[48,192]{1,0:T(8,128)S(1)} %get-tuple-element.52), channel_id=1, source_target_pairs={{0,2},{1,3},{2,0},{3,1},{4,6},{5,7},{6,4},{7,5},{8,10},{9,11},{10,... | collective-permute-start | bytes 110600 | tf_op jit(solution)/shard_map/ppermute | solution.py:35
  70.3 7.5 %collective-permute-start.16 = (f32[48,192]{1,0:T(8,128)S(1)}, f32[48,192]{1,0:T(8,128)S(1)}, u32[]{:S(2)}, u32[]{:S(2)}) collective-permute-start(f32[48,192]{1,0:T(8,128)S(1)} %get-tuple-element.53), channel_id=1, source_target_pairs={{0,3},{1,2},{2,1},{3,0},{4,7},{5,6},{6,5},{7,4},{8,11},{9,10},{10,... | collective-permute-start | bytes 110600 | tf_op jit(solution)/shard_map/ppermute | solution.py:35
  72.9 12.5 %collective-permute-start.13 = (f32[192,384]{1,0:T(8,128)S(1)}, f32[192,384]{1,0:T(8,128)S(1)}, u32[]{:S(2)}, u32[]{:S(2)}) collective-permute-start(f32[192,384]{1,0:T(8,128)S(1)} %shard_map.63.refs_0_), channel_id=1, source_target_pairs={{0,32},{1,33},{2,34},{3,35},{4,36},{5,37},{6,38},{7,39},{8,232},{9... | collective-permute-start | bytes 884744 | tf_op jit(solution)/shard_map/ppermute | solution.py:42
  76.2 9.3 %collective-permute-start.22 = (f32[192,384]{1,0:T(8,128)S(1)}, f32[192,384]{1,0:T(8,128)S(1)}, u32[]{:S(2)}, u32[]{:S(2)}) collective-permute-start(f32[192,384]{1,0:T(8,128)S(1)} %shard_map.63.refs_0_), channel_id=1, source_target_pairs={{0,8},{1,9},{2,10},{3,11},{4,12},{5,13},{6,14},{7,15},{8,0},{9,1},... | collective-permute-start | bytes 884744 | tf_op jit(solution)/shard_map/ppermute | solution.py:35
  77.8 4.8 %collective-permute-start.18 = (f32[48,192]{1,0:T(8,128)S(1)}, f32[48,192]{1,0:T(8,128)S(1)}, u32[]{:S(2)}, u32[]{:S(2)}) collective-permute-start(f32[48,192]{1,0:T(8,128)S(1)} %add_add_fusion.1), channel_id=1, source_target_pairs={{0,16},{1,17},{2,18},{3,19},{4,20},{5,21},{6,22},{7,23},{8,24},{9,... | collective-permute-start | bytes 110600 | tf_op jit(solution)/shard_map/ppermute | solution.py:35
  85.5 6.0 %collective-permute-start.23 = (f32[192,384]{1,0:T(8,128)S(1)}, f32[192,384]{1,0:T(8,128)S(1)}, u32[]{:S(2)}, u32[]{:S(2)}) collective-permute-start(f32[192,384]{1,0:T(8,128)S(1)} %collective-permute-done.22.refs_1_), channel_id=1, source_target_pairs={{0,32},{1,33},{2,34},{3,35},{4,36},{5,37},{6,38},{7,39},{8,232},{9... | collective-permute-start | bytes 884744 | tf_op jit(solution)/shard_map/ppermute | solution.py:42
  87.9 9.0 %collective-permute-start.20 = (f32[216,384]{1,0:T(8,128)S(1)}, f32[216,384]{1,0:T(8,128)S(1)}, u32[]{:S(2)}, u32[]{:S(2)}) collective-permute-start(f32[216,384]{1,0:T(8,128)S(1)} %maximum_maximum_fusion), channel_id=1, source_target_pairs={{0,32},{1,33},{2,34},{3,35},{4,36},{5,37},{6,38},{7,39},{8,232},{9... | collective-permute-start | bytes 995336 | tf_op jit(solution)/shard_map/ppermute | solution.py:42
  91.5 8.4 %collective-permute-start.26 = (f32[216,384]{1,0:T(8,128)S(1)}, f32[216,384]{1,0:T(8,128)S(1)}, u32[]{:S(2)}, u32[]{:S(2)}) collective-permute-start(f32[216,384]{1,0:T(8,128)S(1)} %pad_maximum_fusion.3), channel_id=1, source_target_pairs={{0,32},{1,33},{2,34},{3,35},{4,36},{5,37},{6,38},{7,39},{8,232},{9... | collective-permute-start | bytes 995336 | tf_op jit(solution)/shard_map/ppermute | solution.py:42
  94.8 10.5 %collective-permute-start.24 = (f32[2,192,384]{2,1,0:T(8,128)S(1)}, f32[2,192,384]{2,1,0:T(8,128)S(1)}, u32[]{:S(2)}, u32[]{:S(2)}) collective-permute-start(f32[2,192,384]{2,1,0:T(8,128)S(1)} %pad_maximum_fusion), channel_id=1, source_target_pairs={{0,8},{1,9},{2,10},{3,11},{4,12},{5,13},{6,14},{7,15},{8,0},{9,1},... | collective-permute-start | bytes 1769480 | tf_op jit(solution)/shard_map/ppermute | solution.py:35
  96.9 9.6 %collective-permute-start.21 = (f32[216,384]{1,0:T(8,128)S(1)}, f32[216,384]{1,0:T(8,128)S(1)}, u32[]{:S(2)}, u32[]{:S(2)}) collective-permute-start(f32[216,384]{1,0:T(8,128)S(1)} %collective-permute-done.20.refs_0_), channel_id=1, source_target_pairs={{0,32},{1,33},{2,34},{3,35},{4,36},{5,37},{6,38},{7,39},{8,232},{9... | collective-permute-start | bytes 995336 | tf_op jit(solution)/shard_map/ppermute | solution.py:42
  100.0 11.6 %collective-permute-start.30 = (f32[2,192,384]{2,1,0:T(8,128)S(1)}, f32[2,192,384]{2,1,0:T(8,128)S(1)}, u32[]{:S(2)}, u32[]{:S(2)}) collective-permute-start(f32[2,192,384]{2,1,0:T(8,128)S(1)} %pad_maximum_fusion.2), channel_id=1, source_target_pairs={{0,8},{1,9},{2,10},{3,11},{4,12},{5,13},{6,14},{7,15},{8,0},{9,1},... | collective-permute-start | bytes 1769480 | tf_op jit(solution)/shard_map/ppermute | solution.py:35
  105.3 6.3 %collective-permute-start.27 = (f32[216,384]{1,0:T(8,128)S(1)}, f32[216,384]{1,0:T(8,128)S(1)}, u32[]{:S(2)}, u32[]{:S(2)}) collective-permute-start(f32[216,384]{1,0:T(8,128)S(1)} %collective-permute-done.26.refs_1_), channel_id=1, source_target_pairs={{0,32},{1,33},{2,34},{3,35},{4,36},{5,37},{6,38},{7,39},{8,232},{9... | collective-permute-start | bytes 995336 | tf_op jit(solution)/shard_map/ppermute | solution.py:42
  106.5 8.5 %collective-permute-start.29 = (f32[216,384]{1,0:T(8,128)S(1)}, f32[216,384]{1,0:T(8,128)S(1)}, u32[]{:S(2)}, u32[]{:S(2)}) collective-permute-start(f32[216,384]{1,0:T(8,128)S(1)} %collective-permute-done.21.refs_2_), channel_id=1, source_target_pairs={{0,32},{1,33},{2,34},{3,35},{4,36},{5,37},{6,38},{7,39},{8,232},{9... | collective-permute-start | bytes 995336 | tf_op jit(solution)/shard_map/ppermute | solution.py:42
  118.5 5.7 %collective-permute-start.33 = (f32[48,384]{1,0:T(8,128)S(1)}, f32[48,384]{1,0:T(8,128)S(1)}, u32[]{:S(2)}, u32[]{:S(2)}) collective-permute-start(f32[48,384]{1,0:T(8,128)S(1)} %pad_maximum_fusion.6), channel_id=1, source_target_pairs={{0,8},{1,9},{2,10},{3,11},{4,12},{5,13},{6,14},{7,15},{8,0},{9,1},... | collective-permute-start | bytes 221192 | tf_op jit(solution)/shard_map/ppermute | solution.py:35
  123.3 5.0 %collective-permute-start.28 = (f32[2,192,384]{2,1,0:T(8,128)S(1)}, f32[2,192,384]{2,1,0:T(8,128)S(1)}, u32[]{:S(2)}, u32[]{:S(2)}) collective-permute-start(f32[2,192,384]{2,1,0:T(8,128)S(1)} %pad_maximum_fusion.1), channel_id=1, source_target_pairs={{0,8},{1,9},{2,10},{3,11},{4,12},{5,13},{6,14},{7,15},{8,0},{9,1},... | collective-permute-start | bytes 1769480 | tf_op jit(solution)/shard_map/ppermute | solution.py:35
  123.4 4.8 %collective-permute-start.31 = (f32[216,384]{1,0:T(8,128)S(1)}, f32[216,384]{1,0:T(8,128)S(1)}, u32[]{:S(2)}, u32[]{:S(2)}) collective-permute-start(f32[216,384]{1,0:T(8,128)S(1)} %collective-permute-done.29.refs_1_), channel_id=1, source_target_pairs={{0,8},{1,9},{2,10},{3,11},{4,12},{5,13},{6,14},{7,15},{8,0},{9,1},... | collective-permute-start | bytes 995336 | tf_op jit(solution)/shard_map/ppermute | solution.py:35
  124.3 5.0 %collective-permute-start.34 = (f32[2,48,192]{2,1,0:T(8,128)S(1)}, f32[2,48,192]{2,1,0:T(8,128)S(1)}, u32[]{:S(2)}, u32[]{:S(2)}) collective-permute-start(f32[2,48,192]{2,1,0:T(8,128)S(1)} %pad_maximum_fusion.4), channel_id=1, source_target_pairs={{0,1},{1,0},{2,3},{3,2},{4,5},{5,4},{6,7},{7,6},{8,9},{9,8},{10,11... | collective-permute-start | bytes 221192 | tf_op jit(solution)/shard_map/ppermute | solution.py:35
  124.4 6.6 %collective-permute-start.35 = (f32[2,48,192]{2,1,0:T(8,128)S(1)}, f32[2,48,192]{2,1,0:T(8,128)S(1)}, u32[]{:S(2)}, u32[]{:S(2)}) collective-permute-start(f32[2,48,192]{2,1,0:T(8,128)S(1)} %pad_maximum_fusion.4), channel_id=1, source_target_pairs={{0,2},{1,3},{2,0},{3,1},{4,6},{5,7},{6,4},{7,5},{8,10},{9,11},{10,... | collective-permute-start | bytes 221192 | tf_op jit(solution)/shard_map/ppermute | solution.py:35
  126.3 7.2 %collective-permute-start.36 = (f32[2,48,192]{2,1,0:T(8,128)S(1)}, f32[2,48,192]{2,1,0:T(8,128)S(1)}, u32[]{:S(2)}, u32[]{:S(2)}) collective-permute-start(f32[2,48,192]{2,1,0:T(8,128)S(1)} %pad_maximum_fusion.4), channel_id=1, source_target_pairs={{0,3},{1,2},{2,1},{3,0},{4,7},{5,6},{6,5},{7,4},{8,11},{9,10},{10,... | collective-permute-start | bytes 221192 | tf_op jit(solution)/shard_map/ppermute | solution.py:35
  (10 other events, 45.5 us)

commit v4 on v3

--- a/solution.py
+++ b/solution.py
@@ -225,13 +225,14 @@
     keep1, send1 = product((4, -3), {4: 0}, {}, {-3: 0}, {4: 1, -3: 2}, ainv, left)
     keep2, send2 = product((3, -2, -1), {3: 0}, {3: 1}, {-2: 0, -1: 1}, {-2: 2, -1: 3}, ainv, left)
     keep3, send3 = product((2, 1, 0), {2: 0, 1: 1, 0: 2}, {2: 3, 1: 4}, {}, {0: 0}, ainv, left)
-    got1 = shift(after(send1, facing, keep2, keep3), fc=1)
+    far_own = shift(after(send1[1], facing, keep2, keep3), fc=1)
+    got1 = shift(jnp.stack([send1[0], send1[2]]), fc=1)
     got2 = shift(send2, fc=1)
     got3 = shift(send3, fc=1)
 
     own_part = {
-        4: keep1[0] + got1[1],
-        3: keep2[0] + got1[2],
+        4: keep1[0] + far_own,
+        3: keep2[0] + got1[1],
         2: keep3[0] + got2[2],
         1: keep3[1] + got2[3],
         0: keep3[2] + got3[0],

time: 135 us -> 134 us (level)
    ppermute x21 -> x22, waiting for transfers between devices: 11.9 us -> 11.5 us  [shift(): return lax.ppermute(value, AXES, perm)]
    ppermute x21 -> x22, starting transfers between devices: 37.9 us -> 37.9 us  [shift(): return lax.ppermute(value, AXES, perm)]
  transfers between devices with their start and end apart: 37 -> 38, of which waited for: 16 -> 15; matrix products, arithmetic and copies ran while one was open for 1% -> 1% of each run, Pallas kernels for 8% -> 8%
where the time goes in v4:
time: 134 us
  starting transfers between devices  85.9 us (64%)
  waiting for transfers between devices  26.2 us (20%)
  Pallas kernels  11.2 us (8%)
  local copies, waits for them, and re-layouts  7.03 us (5%)
  other arithmetic  1.97 us (1%)
    ppermute x15, starting transfers between devices, ring(): return lax.ppermute(value, AXES, perm)  41.8 us
    ppermute x22, starting transfers between devices, shift(): return lax.ppermute(value, AXES, perm)  37.9 us
    ppermute x15, waiting for transfers between devices, ring(): return lax.ppermute(value, AXES, perm)  14.7 us
    ppermute x22, waiting for transfers between devices, shift(): return lax.ppermute(value, AXES, perm)  11.5 us
    pallas_call x3, Pallas kernels, product(): pl.pallas_call(functools.partial(product_kernel, chunks, own_keep, other_...  6.82 us
    ppermute x1, starting transfers between devices, local(): facing = lax.ppermute(give, AXES, perm)  6.29 us
    unnamed x10, local copies, waits for them, and re-layouts  5.63 us
    pallas_call x3, Pallas kernels, put(): pl.pallas_call(functools.partial(put_kernel, pieces, out is not None), ou...  3.59 us
  transfers between devices with their start and end apart: 38, of which 15 were waited for; matrix products, arithmetic and copies ran while one was open for 1% of the time, Pallas kernels for 8%

profile of v4, /device:TPU:1, one launch (start us, length us, event | category | flops | bytes accessed | tf_op | source)
XLA Modules:
  0.0 133.7 jit_solution(1696138146752752723)
XLA Ops:
  1.7 6.3 %collective-permute-start.7 = (f32[192,384]{1,0:T(8,128)S(1)}, f32[192,384]{1,0:T(8,128)S(1)}, u32[]{:S(2)}, u32[]{:S(2)}) collective-permute-start(f32[192,384]{1,0:T(8,128)S(1)} %dynamic-slice_bitcast_fusion), channel_id=1, source_target_pairs={{0,0},{1,8},{2,16},{3,24},{4,32},{5,40},{6,48},{7,56},{8,64},{9,72... | collective-permute-start | bytes 884744 | tf_op jit(solution)/shard_map/ppermute | solution.py:222
  10.6 3.7 %copy-done = f32[768,3072]{1,0:T(8,128)S(1)} copy-done((f32[768,3072]{1,0:T(8,128)S(1)}, f32[768,3072]{1,0:T(8,128)}, u32[]{:S(2)}) %copy-start) | copy-done | bytes 9437208
  14.3 2.6 %shard_map.61 = (f32[2,192,384]{2,1,0:T(8,128)S(1)}, f32[4,192,384]{2,1,0:T(8,128)S(1)}) custom-call(bf16[768,768]{1,0:T(8,128)(2,1)S(1)} %shard_map.59.left, f32[768,3072]{1,0:T(8,128)S(1)} %copy-done), custom_call_target="tpu_custom_call" | custom-call | flops 1000 | bytes 1000 | tf_op jit(solution)/shard_map/pallas_call | solution.py:139
  17.0 1.6 %shard_map.62 = (f32[1,192,384]{2,1,0:T(8,128)S(1)}, f32[3,192,384]{2,1,0:T(8,128)S(1)}) custom-call(bf16[768,768]{1,0:T(8,128)(2,1)S(1)} %shard_map.59.left, f32[768,3072]{1,0:T(8,128)S(1)} %copy-done), custom_call_target="tpu_custom_call" | custom-call | flops 1000 | bytes 1000 | tf_op jit(solution)/shard_map/pallas_call | solution.py:139
  19.3 2.6 %shard_map.60 = (f32[5,192,384]{2,1,0:T(8,128)S(1)}, f32[1,192,384]{2,1,0:T(8,128)S(1)}) custom-call(bf16[768,768]{1,0:T(8,128)(2,1)S(1)} %shard_map.59.left, f32[768,3072]{1,0:T(8,128)S(1)} %copy-done), custom_call_target="tpu_custom_call" | custom-call | flops 1000 | bytes 1000 | tf_op jit(solution)/shard_map/pallas_call | solution.py:139
  22.0 1.6 %collective-permute-done.8 = f32[192,384]{1,0:T(8,128)S(1)} collective-permute-done((f32[192,384]{1,0:T(8,128)S(1)}, f32[192,384]{1,0:T(8,128)S(1)}, u32[]{:S(2)}, u32[]{:S(2)}) %collective-permute-start.8) | collective-permute-done | bytes 294944 | tf_op jit(solution)/shard_map/ppermute | solution.py:35
  23.6 12.6 %collective-permute-start.9 = (f32[192,384]{1,0:T(8,128)S(1)}, f32[192,384]{1,0:T(8,128)S(1)}, u32[]{:S(2)}, u32[]{:S(2)}) collective-permute-start(f32[192,384]{1,0:T(8,128)S(1)} %bitcast_add_fusion), channel_id=1, source_target_pairs={{0,32},{1,33},{2,34},{3,35},{4,36},{5,37},{6,38},{7,39},{8,232},{9... | collective-permute-start | bytes 884744 | tf_op jit(solution)/shard_map/ppermute | solution.py:42
  36.5 3.3 %collective-permute-done.9 = f32[192,384]{1,0:T(8,128)S(1)} collective-permute-done((f32[192,384]{1,0:T(8,128)S(1)}, f32[192,384]{1,0:T(8,128)S(1)}, u32[]{:S(2)}, u32[]{:S(2)}) %collective-permute-start.9) | collective-permute-done | bytes 294944 | tf_op jit(solution)/shard_map/ppermute | solution.py:42
  39.9 3.2 %collective-permute-start.10 = (f32[192,384]{1,0:T(8,128)S(1)}, f32[192,384]{1,0:T(8,128)S(1)}, u32[]{:S(2)}, u32[]{:S(2)}) collective-permute-start(f32[192,384]{1,0:T(8,128)S(1)} %add.181), channel_id=1, source_target_pairs={{0,32},{1,33},{2,34},{3,35},{4,36},{5,37},{6,38},{7,39},{8,232},{9... | collective-permute-start | bytes 884744 | tf_op jit(solution)/shard_map/ppermute | solution.py:42
  43.3 2.9 %collective-permute-start.4 = (f32[192,384]{1,0:T(8,128)S(1)}, f32[192,384]{1,0:T(8,128)S(1)}, u32[]{:S(2)}, u32[]{:S(2)}) collective-permute-start(f32[192,384]{1,0:T(8,128)S(1)} %add.168), channel_id=1, source_target_pairs={{0,32},{1,33},{2,34},{3,35},{4,36},{5,37},{6,38},{7,39},{8,232},{9... | collective-permute-start | bytes 884744 | tf_op jit(solution)/shard_map/ppermute | solution.py:42
  46.7 3.4 %collective-permute-start.11 = (f32[192,384]{1,0:T(8,128)S(1)}, f32[192,384]{1,0:T(8,128)S(1)}, u32[]{:S(2)}, u32[]{:S(2)}) collective-permute-start(f32[192,384]{1,0:T(8,128)S(1)} %add.182), channel_id=1, source_target_pairs={{0,32},{1,33},{2,34},{3,35},{4,36},{5,37},{6,38},{7,39},{8,232},{9... | collective-permute-start | bytes 884744 | tf_op jit(solution)/shard_map/ppermute | solution.py:42
  50.2 3.0 %collective-permute-start.5 = (f32[192,384]{1,0:T(8,128)S(1)}, f32[192,384]{1,0:T(8,128)S(1)}, u32[]{:S(2)}, u32[]{:S(2)}) collective-permute-start(f32[192,384]{1,0:T(8,128)S(1)} %add.169), channel_id=1, source_target_pairs={{0,32},{1,33},{2,34},{3,35},{4,36},{5,37},{6,38},{7,39},{8,232},{9... | collective-permute-start | bytes 884744 | tf_op jit(solution)/shard_map/ppermute | solution.py:42
  53.8 3.2 %collective-permute-start.12 = (f32[192,384]{1,0:T(8,128)S(1)}, f32[192,384]{1,0:T(8,128)S(1)}, u32[]{:S(2)}, u32[]{:S(2)}) collective-permute-start(f32[192,384]{1,0:T(8,128)S(1)} %add.183), channel_id=1, source_target_pairs={{0,32},{1,33},{2,34},{3,35},{4,36},{5,37},{6,38},{7,39},{8,232},{9... | collective-permute-start | bytes 884744 | tf_op jit(solution)/shard_map/ppermute | solution.py:42
  57.0 3.8 %collective-permute-start.6 = (f32[192,384]{1,0:T(8,128)S(1)}, f32[192,384]{1,0:T(8,128)S(1)}, u32[]{:S(2)}, u32[]{:S(2)}) collective-permute-start(f32[192,384]{1,0:T(8,128)S(1)} %collective-permute-done.5), channel_id=1, source_target_pairs={{0,8},{1,9},{2,10},{3,11},{4,12},{5,13},{6,14},{7,15},{8,0},{9,1},... | collective-permute-start | bytes 884744 | tf_op jit(solution)/shard_map/ppermute | solution.py:35
  62.1 5.5 %collective-permute-start.13 = (f32[192,384]{1,0:T(8,128)S(1)}, f32[192,384]{1,0:T(8,128)S(1)}, u32[]{:S(2)}, u32[]{:S(2)}) collective-permute-start(f32[192,384]{1,0:T(8,128)S(1)} %add_multiply_fusion.a_ref), channel_id=1, source_target_pairs={{0,16},{1,17},{2,18},{3,19},{4,20},{5,21},{6,22},{7,23},{8,24},{9,... | collective-permute-start | bytes 884744 | tf_op jit(solution)/shard_map/ppermute | solution.py:35
  69.3 2.6 %collective-permute-start.17 = (f32[48,192]{1,0:T(8,128)S(1)}, f32[48,192]{1,0:T(8,128)S(1)}, u32[]{:S(2)}, u32[]{:S(2)}) collective-permute-start(f32[48,192]{1,0:T(8,128)S(1)} %get-tuple-element.55), channel_id=1, source_target_pairs={{0,3},{1,2},{2,1},{3,0},{4,7},{5,6},{6,5},{7,4},{8,11},{9,10},{10,... | collective-permute-start | bytes 110600 | tf_op jit(solution)/shard_map/ppermute | solution.py:35
  72.0 3.4 %collective-permute-start.14 = (f32[192,384]{1,0:T(8,128)S(1)}, f32[192,384]{1,0:T(8,128)S(1)}, u32[]{:S(2)}, u32[]{:S(2)}) collective-permute-start(f32[192,384]{1,0:T(8,128)S(1)} %shard_map.63.refs_0_), channel_id=1, source_target_pairs={{0,32},{1,33},{2,34},{3,35},{4,36},{5,37},{6,38},{7,39},{8,232},{9... | collective-permute-start | bytes 884744 | tf_op jit(solution)/shard_map/ppermute | solution.py:42
  77.1 2.9 %collective-permute-start.19 = (f32[48,192]{1,0:T(8,128)S(1)}, f32[48,192]{1,0:T(8,128)S(1)}, u32[]{:S(2)}, u32[]{:S(2)}) collective-permute-start(f32[48,192]{1,0:T(8,128)S(1)} %add_add_fusion.1), channel_id=1, source_target_pairs={{0,16},{1,17},{2,18},{3,19},{4,20},{5,21},{6,22},{7,23},{8,24},{9,... | collective-permute-start | bytes 110600 | tf_op jit(solution)/shard_map/ppermute | solution.py:35
  81.9 2.8 %collective-permute-done.20 = f32[48,192]{1,0:T(8,128)S(1)} collective-permute-done((f32[48,192]{1,0:T(8,128)S(1)}, f32[48,192]{1,0:T(8,128)S(1)}, u32[]{:S(2)}, u32[]{:S(2)}) %collective-permute-start.20) | collective-permute-done | bytes 36896 | tf_op jit(solution)/shard_map/ppermute | solution.py:35
  84.7 2.4 %collective-permute-start.24 = (f32[192,384]{1,0:T(8,128)S(1)}, f32[192,384]{1,0:T(8,128)S(1)}, u32[]{:S(2)}, u32[]{:S(2)}) collective-permute-start(f32[192,384]{1,0:T(8,128)S(1)} %collective-permute-done.23.refs_1_), channel_id=1, source_target_pairs={{0,32},{1,33},{2,34},{3,35},{4,36},{5,37},{6,38},{7,39},{8,232},{9... | collective-permute-start | bytes 884744 | tf_op jit(solution)/shard_map/ppermute | solution.py:42
  90.8 3.2 %collective-permute-start.27 = (f32[216,384]{1,0:T(8,128)S(1)}, f32[216,384]{1,0:T(8,128)S(1)}, u32[]{:S(2)}, u32[]{:S(2)}) collective-permute-start(f32[216,384]{1,0:T(8,128)S(1)} %pad_maximum_fusion.4), channel_id=1, source_target_pairs={{0,32},{1,33},{2,34},{3,35},{4,36},{5,37},{6,38},{7,39},{8,232},{9... | collective-permute-start | bytes 995336 | tf_op jit(solution)/shard_map/ppermute | solution.py:42
  94.0 2.2 %collective-permute-start.25 = (f32[2,192,384]{2,1,0:T(8,128)S(1)}, f32[2,192,384]{2,1,0:T(8,128)S(1)}, u32[]{:S(2)}, u32[]{:S(2)}) collective-permute-start(f32[2,192,384]{2,1,0:T(8,128)S(1)} %pad_maximum_fusion.1), channel_id=1, source_target_pairs={{0,8},{1,9},{2,10},{3,11},{4,12},{5,13},{6,14},{7,15},{8,0},{9,1},... | collective-permute-start | bytes 1769480 | tf_op jit(solution)/shard_map/ppermute | solution.py:35
  96.2 2.9 %collective-permute-start.22 = (f32[216,384]{1,0:T(8,128)S(1)}, f32[216,384]{1,0:T(8,128)S(1)}, u32[]{:S(2)}, u32[]{:S(2)}) collective-permute-start(f32[216,384]{1,0:T(8,128)S(1)} %collective-permute-done.21.refs_0_), channel_id=1, source_target_pairs={{0,32},{1,33},{2,34},{3,35},{4,36},{5,37},{6,38},{7,39},{8,232},{9... | collective-permute-start | bytes 995336 | tf_op jit(solution)/shard_map/ppermute | solution.py:42
  99.3 5.5 %collective-permute-start.31 = (f32[2,192,384]{2,1,0:T(8,128)S(1)}, f32[2,192,384]{2,1,0:T(8,128)S(1)}, u32[]{:S(2)}, u32[]{:S(2)}) collective-permute-start(f32[2,192,384]{2,1,0:T(8,128)S(1)} %pad_maximum_fusion.3), channel_id=1, source_target_pairs={{0,8},{1,9},{2,10},{3,11},{4,12},{5,13},{6,14},{7,15},{8,0},{9,1},... | collective-permute-start | bytes 1769480 | tf_op jit(solution)/shard_map/ppermute | solution.py:35
  106.3 4.7 %collective-permute-done.28.refs_3_ = f32[216,384]{1,0:T(8,128)S(1)} collective-permute-done((f32[216,384]{1,0:T(8,128)S(1)}, f32[216,384]{1,0:T(8,128)S(1)}, u32[]{:S(2)}, u32[]{:S(2)}) %collective-permute-start.28) | collective-permute-done | bytes 331808 | tf_op jit(solution)/shard_map/ppermute | solution.py:42
  112.3 2.3 %collective-permute-done.30.refs_1_ = f32[216,384]{1,0:T(8,128)S(1)} collective-permute-done((f32[216,384]{1,0:T(8,128)S(1)}, f32[216,384]{1,0:T(8,128)S(1)}, u32[]{:S(2)}, u32[]{:S(2)}) %collective-permute-start.30) | collective-permute-done | bytes 331808 | tf_op jit(solution)/shard_map/ppermute | solution.py:42
  115.6 2.3 %collective-permute-done.33 = f32[48,384]{1,0:T(8,128)S(1)} collective-permute-done((f32[48,384]{1,0:T(8,128)S(1)}, f32[48,384]{1,0:T(8,128)S(1)}, u32[]{:S(2)}, u32[]{:S(2)}) %collective-permute-start.33) | collective-permute-done | bytes 73760 | tf_op jit(solution)/shard_map/ppermute | solution.py:42
  118.0 4.6 %collective-permute-start.34 = (f32[48,384]{1,0:T(8,128)S(1)}, f32[48,384]{1,0:T(8,128)S(1)}, u32[]{:S(2)}, u32[]{:S(2)}) collective-permute-start(f32[48,384]{1,0:T(8,128)S(1)} %pad_maximum_fusion.7), channel_id=1, source_target_pairs={{0,8},{1,9},{2,10},{3,11},{4,12},{5,13},{6,14},{7,15},{8,0},{9,1},... | collective-permute-start | bytes 221192 | tf_op jit(solution)/shard_map/ppermute | solution.py:35
  123.7 1.9 %collective-permute-start.36 = (f32[2,48,192]{2,1,0:T(8,128)S(1)}, f32[2,48,192]{2,1,0:T(8,128)S(1)}, u32[]{:S(2)}, u32[]{:S(2)}) collective-permute-start(f32[2,48,192]{2,1,0:T(8,128)S(1)} %pad_maximum_fusion.5), channel_id=1, source_target_pairs={{0,2},{1,3},{2,0},{3,1},{4,6},{5,7},{6,4},{7,5},{8,10},{9,11},{10,... | collective-permute-start | bytes 221192 | tf_op jit(solution)/shard_map/ppermute | solution.py:35
  125.6 1.9 %collective-permute-start.37 = (f32[2,48,192]{2,1,0:T(8,128)S(1)}, f32[2,48,192]{2,1,0:T(8,128)S(1)}, u32[]{:S(2)}, u32[]{:S(2)}) collective-permute-start(f32[2,48,192]{2,1,0:T(8,128)S(1)} %pad_maximum_fusion.5), channel_id=1, source_target_pairs={{0,3},{1,2},{2,1},{3,0},{4,7},{5,6},{6,5},{7,4},{8,11},{9,10},{10,... | collective-permute-start | bytes 221192 | tf_op jit(solution)/shard_map/ppermute | solution.py:35
  128.7 1.6 %collective-permute-done.36 = f32[2,48,192]{2,1,0:T(8,128)S(1)} collective-permute-done((f32[2,48,192]{2,1,0:T(8,128)S(1)}, f32[2,48,192]{2,1,0:T(8,128)S(1)}, u32[]{:S(2)}, u32[]{:S(2)}) %collective-permute-start.36) | collective-permute-done | bytes 73760 | tf_op jit(solution)/shard_map/ppermute | solution.py:35
  130.3 2.6 %collective-permute-done.37 = f32[2,48,192]{2,1,0:T(8,128)S(1)} collective-permute-done((f32[2,48,192]{2,1,0:T(8,128)S(1)}, f32[2,48,192]{2,1,0:T(8,128)S(1)}, u32[]{:S(2)}, u32[]{:S(2)}) %collective-permute-start.37) | collective-permute-done | bytes 73760 | tf_op jit(solution)/shard_map/ppermute | solution.py:35
  (106 shorter events, 23.8 us)
Async XLA Ops:
  1.7 20.2 %collective-permute-start.7 = (f32[192,384]{1,0:T(8,128)S(1)}, f32[192,384]{1,0:T(8,128)S(1)}, u32[]{:S(2)}, u32[]{:S(2)}) collective-permute-start(f32[192,384]{1,0:T(8,128)S(1)} %dynamic-slice_bitcast_fusion), channel_id=1, source_target_pairs={{0,0},{1,8},{2,16},{3,24},{4,32},{5,40},{6,48},{7,56},{8,64},{9,72... | collective-permute-start | bytes 884744 | tf_op jit(solution)/shard_map/ppermute | solution.py:222
  16.9 26.2 %collective-permute-start.1 = (f32[4,192,384]{2,1,0:T(8,128)S(1)}, f32[4,192,384]{2,1,0:T(8,128)S(1)}, u32[]{:S(2)}, u32[]{:S(2)}) collective-permute-start(f32[4,192,384]{2,1,0:T(8,128)S(1)} %get-tuple-element.23), channel_id=1, source_target_pairs={{0,8},{1,9},{2,10},{3,11},{4,12},{5,13},{6,14},{7,15},{8,0},{9,1},... | collective-permute-start | bytes 3538952 | tf_op jit(solution)/shard_map/ppermute | solution.py:35
  18.8 17.4 %collective-permute-start.2 = (f32[2,192,384]{2,1,0:T(8,128)S(1)}, f32[2,192,384]{2,1,0:T(8,128)S(1)}, u32[]{:S(2)}, u32[]{:S(2)}) collective-permute-start(f32[2,192,384]{2,1,0:T(8,128)S(1)} %pad_maximum_fusion), channel_id=1, source_target_pairs={{0,8},{1,9},{2,10},{3,11},{4,12},{5,13},{6,14},{7,15},{8,0},{9,1},... | collective-permute-start | bytes 1769480 | tf_op jit(solution)/shard_map/ppermute | solution.py:35
  23.6 16.2 %collective-permute-start.9 = (f32[192,384]{1,0:T(8,128)S(1)}, f32[192,384]{1,0:T(8,128)S(1)}, u32[]{:S(2)}, u32[]{:S(2)}) collective-permute-start(f32[192,384]{1,0:T(8,128)S(1)} %bitcast_add_fusion), channel_id=1, source_target_pairs={{0,32},{1,33},{2,34},{3,35},{4,36},{5,37},{6,38},{7,39},{8,232},{9... | collective-permute-start | bytes 884744 | tf_op jit(solution)/shard_map/ppermute | solution.py:42
  36.1 6.9 %collective-permute-start = (f32[1,192,384]{2,1,0:T(8,128)S(1)}, f32[1,192,384]{2,1,0:T(8,128)S(1)}, u32[]{:S(2)}, u32[]{:S(2)}) collective-permute-start(f32[1,192,384]{2,1,0:T(8,128)S(1)} %get-tuple-element.22), channel_id=1, source_target_pairs={{0,8},{1,9},{2,10},{3,11},{4,12},{5,13},{6,14},{7,15},{8,0},{9,1},... | collective-permute-start | bytes 884744 | tf_op jit(solution)/shard_map/ppermute | solution.py:35
  36.2 7.0 %collective-permute-start.3 = (f32[192,384]{1,0:T(8,128)S(1)}, f32[192,384]{1,0:T(8,128)S(1)}, u32[]{:S(2)}, u32[]{:S(2)}) collective-permute-start(f32[192,384]{1,0:T(8,128)S(1)} %get-tuple-element.45), channel_id=1, source_target_pairs={{0,32},{1,33},{2,34},{3,35},{4,36},{5,37},{6,38},{7,39},{8,232},{9... | collective-permute-start | bytes 884744 | tf_op jit(solution)/shard_map/ppermute | solution.py:42
  39.9 6.9 %collective-permute-start.10 = (f32[192,384]{1,0:T(8,128)S(1)}, f32[192,384]{1,0:T(8,128)S(1)}, u32[]{:S(2)}, u32[]{:S(2)}) collective-permute-start(f32[192,384]{1,0:T(8,128)S(1)} %add.181), channel_id=1, source_target_pairs={{0,32},{1,33},{2,34},{3,35},{4,36},{5,37},{6,38},{7,39},{8,232},{9... | collective-permute-start | bytes 884744 | tf_op jit(solution)/shard_map/ppermute | solution.py:42
  43.3 6.9 %collective-permute-start.4 = (f32[192,384]{1,0:T(8,128)S(1)}, f32[192,384]{1,0:T(8,128)S(1)}, u32[]{:S(2)}, u32[]{:S(2)}) collective-permute-start(f32[192,384]{1,0:T(8,128)S(1)} %add.168), channel_id=1, source_target_pairs={{0,32},{1,33},{2,34},{3,35},{4,36},{5,37},{6,38},{7,39},{8,232},{9... | collective-permute-start | bytes 884744 | tf_op jit(solution)/shard_map/ppermute | solution.py:42
  46.7 7.0 %collective-permute-start.11 = (f32[192,384]{1,0:T(8,128)S(1)}, f32[192,384]{1,0:T(8,128)S(1)}, u32[]{:S(2)}, u32[]{:S(2)}) collective-permute-start(f32[192,384]{1,0:T(8,128)S(1)} %add.182), channel_id=1, source_target_pairs={{0,32},{1,33},{2,34},{3,35},{4,36},{5,37},{6,38},{7,39},{8,232},{9... | collective-permute-start | bytes 884744 | tf_op jit(solution)/shard_map/ppermute | solution.py:42
  50.2 6.9 %collective-permute-start.5 = (f32[192,384]{1,0:T(8,128)S(1)}, f32[192,384]{1,0:T(8,128)S(1)}, u32[]{:S(2)}, u32[]{:S(2)}) collective-permute-start(f32[192,384]{1,0:T(8,128)S(1)} %add.169), channel_id=1, source_target_pairs={{0,32},{1,33},{2,34},{3,35},{4,36},{5,37},{6,38},{7,39},{8,232},{9... | collective-permute-start | bytes 884744 | tf_op jit(solution)/shard_map/ppermute | solution.py:42
  53.8 7.4 %collective-permute-start.12 = (f32[192,384]{1,0:T(8,128)S(1)}, f32[192,384]{1,0:T(8,128)S(1)}, u32[]{:S(2)}, u32[]{:S(2)}) collective-permute-start(f32[192,384]{1,0:T(8,128)S(1)} %add.183), channel_id=1, source_target_pairs={{0,32},{1,33},{2,34},{3,35},{4,36},{5,37},{6,38},{7,39},{8,232},{9... | collective-permute-start | bytes 884744 | tf_op jit(solution)/shard_map/ppermute | solution.py:42
  57.0 5.0 %collective-permute-start.6 = (f32[192,384]{1,0:T(8,128)S(1)}, f32[192,384]{1,0:T(8,128)S(1)}, u32[]{:S(2)}, u32[]{:S(2)}) collective-permute-start(f32[192,384]{1,0:T(8,128)S(1)} %collective-permute-done.5), channel_id=1, source_target_pairs={{0,8},{1,9},{2,10},{3,11},{4,12},{5,13},{6,14},{7,15},{8,0},{9,1},... | collective-permute-start | bytes 884744 | tf_op jit(solution)/shard_map/ppermute | solution.py:35
  62.1 9.8 %collective-permute-start.13 = (f32[192,384]{1,0:T(8,128)S(1)}, f32[192,384]{1,0:T(8,128)S(1)}, u32[]{:S(2)}, u32[]{:S(2)}) collective-permute-start(f32[192,384]{1,0:T(8,128)S(1)} %add_multiply_fusion.a_ref), channel_id=1, source_target_pairs={{0,16},{1,17},{2,18},{3,19},{4,20},{5,21},{6,22},{7,23},{8,24},{9,... | collective-permute-start | bytes 884744 | tf_op jit(solution)/shard_map/ppermute | solution.py:35
  68.0 9.0 %collective-permute-start.15 = (f32[48,192]{1,0:T(8,128)S(1)}, f32[48,192]{1,0:T(8,128)S(1)}, u32[]{:S(2)}, u32[]{:S(2)}) collective-permute-start(f32[48,192]{1,0:T(8,128)S(1)} %get-tuple-element.56), channel_id=1, source_target_pairs={{0,1},{1,0},{2,3},{3,2},{4,5},{5,4},{6,7},{7,6},{8,9},{9,8},{10,11... | collective-permute-start | bytes 110600 | tf_op jit(solution)/shard_map/ppermute | solution.py:35
  68.1 8.9 %collective-permute-start.16 = (f32[48,192]{1,0:T(8,128)S(1)}, f32[48,192]{1,0:T(8,128)S(1)}, u32[]{:S(2)}, u32[]{:S(2)}) collective-permute-start(f32[48,192]{1,0:T(8,128)S(1)} %get-tuple-element.54), channel_id=1, source_target_pairs={{0,2},{1,3},{2,0},{3,1},{4,6},{5,7},{6,4},{7,5},{8,10},{9,11},{10,... | collective-permute-start | bytes 110600 | tf_op jit(solution)/shard_map/ppermute | solution.py:35
  69.3 7.7 %collective-permute-start.17 = (f32[48,192]{1,0:T(8,128)S(1)}, f32[48,192]{1,0:T(8,128)S(1)}, u32[]{:S(2)}, u32[]{:S(2)}) collective-permute-start(f32[48,192]{1,0:T(8,128)S(1)} %get-tuple-element.55), channel_id=1, source_target_pairs={{0,3},{1,2},{2,1},{3,0},{4,7},{5,6},{6,5},{7,4},{8,11},{9,10},{10,... | collective-permute-start | bytes 110600 | tf_op jit(solution)/shard_map/ppermute | solution.py:35
  72.0 12.7 %collective-permute-start.14 = (f32[192,384]{1,0:T(8,128)S(1)}, f32[192,384]{1,0:T(8,128)S(1)}, u32[]{:S(2)}, u32[]{:S(2)}) collective-permute-start(f32[192,384]{1,0:T(8,128)S(1)} %shard_map.63.refs_0_), channel_id=1, source_target_pairs={{0,32},{1,33},{2,34},{3,35},{4,36},{5,37},{6,38},{7,39},{8,232},{9... | collective-permute-start | bytes 884744 | tf_op jit(solution)/shard_map/ppermute | solution.py:42
  75.4 9.3 %collective-permute-start.23 = (f32[192,384]{1,0:T(8,128)S(1)}, f32[192,384]{1,0:T(8,128)S(1)}, u32[]{:S(2)}, u32[]{:S(2)}) collective-permute-start(f32[192,384]{1,0:T(8,128)S(1)} %shard_map.63.refs_0_), channel_id=1, source_target_pairs={{0,8},{1,9},{2,10},{3,11},{4,12},{5,13},{6,14},{7,15},{8,0},{9,1},... | collective-permute-start | bytes 884744 | tf_op jit(solution)/shard_map/ppermute | solution.py:35
  84.7 6.0 %collective-permute-start.24 = (f32[192,384]{1,0:T(8,128)S(1)}, f32[192,384]{1,0:T(8,128)S(1)}, u32[]{:S(2)}, u32[]{:S(2)}) collective-permute-start(f32[192,384]{1,0:T(8,128)S(1)} %collective-permute-done.23.refs_1_), channel_id=1, source_target_pairs={{0,32},{1,33},{2,34},{3,35},{4,36},{5,37},{6,38},{7,39},{8,232},{9... | collective-permute-start | bytes 884744 | tf_op jit(solution)/shard_map/ppermute | solution.py:42
  87.2 9.0 %collective-permute-start.21 = (f32[216,384]{1,0:T(8,128)S(1)}, f32[216,384]{1,0:T(8,128)S(1)}, u32[]{:S(2)}, u32[]{:S(2)}) collective-permute-start(f32[216,384]{1,0:T(8,128)S(1)} %maximum_maximum_fusion), channel_id=1, source_target_pairs={{0,32},{1,33},{2,34},{3,35},{4,36},{5,37},{6,38},{7,39},{8,232},{9... | collective-permute-start | bytes 995336 | tf_op jit(solution)/shard_map/ppermute | solution.py:42
  90.8 8.4 %collective-permute-start.27 = (f32[216,384]{1,0:T(8,128)S(1)}, f32[216,384]{1,0:T(8,128)S(1)}, u32[]{:S(2)}, u32[]{:S(2)}) collective-permute-start(f32[216,384]{1,0:T(8,128)S(1)} %pad_maximum_fusion.4), channel_id=1, source_target_pairs={{0,32},{1,33},{2,34},{3,35},{4,36},{5,37},{6,38},{7,39},{8,232},{9... | collective-permute-start | bytes 995336 | tf_op jit(solution)/shard_map/ppermute | solution.py:42
  94.0 10.7 %collective-permute-start.25 = (f32[2,192,384]{2,1,0:T(8,128)S(1)}, f32[2,192,384]{2,1,0:T(8,128)S(1)}, u32[]{:S(2)}, u32[]{:S(2)}) collective-permute-start(f32[2,192,384]{2,1,0:T(8,128)S(1)} %pad_maximum_fusion.1), channel_id=1, source_target_pairs={{0,8},{1,9},{2,10},{3,11},{4,12},{5,13},{6,14},{7,15},{8,0},{9,1},... | collective-permute-start | bytes 1769480 | tf_op jit(solution)/shard_map/ppermute | solution.py:35
  96.2 9.8 %collective-permute-start.22 = (f32[216,384]{1,0:T(8,128)S(1)}, f32[216,384]{1,0:T(8,128)S(1)}, u32[]{:S(2)}, u32[]{:S(2)}) collective-permute-start(f32[216,384]{1,0:T(8,128)S(1)} %collective-permute-done.21.refs_0_), channel_id=1, source_target_pairs={{0,32},{1,33},{2,34},{3,35},{4,36},{5,37},{6,38},{7,39},{8,232},{9... | collective-permute-start | bytes 995336 | tf_op jit(solution)/shard_map/ppermute | solution.py:42
  99.3 11.8 %collective-permute-start.31 = (f32[2,192,384]{2,1,0:T(8,128)S(1)}, f32[2,192,384]{2,1,0:T(8,128)S(1)}, u32[]{:S(2)}, u32[]{:S(2)}) collective-permute-start(f32[2,192,384]{2,1,0:T(8,128)S(1)} %pad_maximum_fusion.3), channel_id=1, source_target_pairs={{0,8},{1,9},{2,10},{3,11},{4,12},{5,13},{6,14},{7,15},{8,0},{9,1},... | collective-permute-start | bytes 1769480 | tf_op jit(solution)/shard_map/ppermute | solution.py:35
  104.8 6.3 %collective-permute-start.28 = (f32[216,384]{1,0:T(8,128)S(1)}, f32[216,384]{1,0:T(8,128)S(1)}, u32[]{:S(2)}, u32[]{:S(2)}) collective-permute-start(f32[216,384]{1,0:T(8,128)S(1)} %collective-permute-done.27.refs_1_), channel_id=1, source_target_pairs={{0,32},{1,33},{2,34},{3,35},{4,36},{5,37},{6,38},{7,39},{8,232},{9... | collective-permute-start | bytes 995336 | tf_op jit(solution)/shard_map/ppermute | solution.py:42
  106.0 8.5 %collective-permute-start.30 = (f32[216,384]{1,0:T(8,128)S(1)}, f32[216,384]{1,0:T(8,128)S(1)}, u32[]{:S(2)}, u32[]{:S(2)}) collective-permute-start(f32[216,384]{1,0:T(8,128)S(1)} %collective-permute-done.22.refs_2_), channel_id=1, source_target_pairs={{0,32},{1,33},{2,34},{3,35},{4,36},{5,37},{6,38},{7,39},{8,232},{9... | collective-permute-start | bytes 995336 | tf_op jit(solution)/shard_map/ppermute | solution.py:42
  118.0 5.5 %collective-permute-start.34 = (f32[48,384]{1,0:T(8,128)S(1)}, f32[48,384]{1,0:T(8,128)S(1)}, u32[]{:S(2)}, u32[]{:S(2)}) collective-permute-start(f32[48,384]{1,0:T(8,128)S(1)} %pad_maximum_fusion.7), channel_id=1, source_target_pairs={{0,8},{1,9},{2,10},{3,11},{4,12},{5,13},{6,14},{7,15},{8,0},{9,1},... | collective-permute-start | bytes 221192 | tf_op jit(solution)/shard_map/ppermute | solution.py:35
  122.6 5.0 %collective-permute-start.29 = (f32[2,192,384]{2,1,0:T(8,128)S(1)}, f32[2,192,384]{2,1,0:T(8,128)S(1)}, u32[]{:S(2)}, u32[]{:S(2)}) collective-permute-start(f32[2,192,384]{2,1,0:T(8,128)S(1)} %pad_maximum_fusion.2), channel_id=1, source_target_pairs={{0,8},{1,9},{2,10},{3,11},{4,12},{5,13},{6,14},{7,15},{8,0},{9,1},... | collective-permute-start | bytes 1769480 | tf_op jit(solution)/shard_map/ppermute | solution.py:35
  122.7 4.8 %collective-permute-start.32 = (f32[216,384]{1,0:T(8,128)S(1)}, f32[216,384]{1,0:T(8,128)S(1)}, u32[]{:S(2)}, u32[]{:S(2)}) collective-permute-start(f32[216,384]{1,0:T(8,128)S(1)} %collective-permute-done.30.refs_1_), channel_id=1, source_target_pairs={{0,8},{1,9},{2,10},{3,11},{4,12},{5,13},{6,14},{7,15},{8,0},{9,1},... | collective-permute-start | bytes 995336 | tf_op jit(solution)/shard_map/ppermute | solution.py:35
  123.6 5.0 %collective-permute-start.35 = (f32[2,48,192]{2,1,0:T(8,128)S(1)}, f32[2,48,192]{2,1,0:T(8,128)S(1)}, u32[]{:S(2)}, u32[]{:S(2)}) collective-permute-start(f32[2,48,192]{2,1,0:T(8,128)S(1)} %pad_maximum_fusion.5), channel_id=1, source_target_pairs={{0,1},{1,0},{2,3},{3,2},{4,5},{5,4},{6,7},{7,6},{8,9},{9,8},{10,11... | collective-permute-start | bytes 221192 | tf_op jit(solution)/shard_map/ppermute | solution.py:35
  123.7 6.6 %collective-permute-start.36 = (f32[2,48,192]{2,1,0:T(8,128)S(1)}, f32[2,48,192]{2,1,0:T(8,128)S(1)}, u32[]{:S(2)}, u32[]{:S(2)}) collective-permute-start(f32[2,48,192]{2,1,0:T(8,128)S(1)} %pad_maximum_fusion.5), channel_id=1, source_target_pairs={{0,2},{1,3},{2,0},{3,1},{4,6},{5,7},{6,4},{7,5},{8,10},{9,11},{10,... | collective-permute-start | bytes 221192 | tf_op jit(solution)/shard_map/ppermute | solution.py:35
  125.6 7.2 %collective-permute-start.37 = (f32[2,48,192]{2,1,0:T(8,128)S(1)}, f32[2,48,192]{2,1,0:T(8,128)S(1)}, u32[]{:S(2)}, u32[]{:S(2)}) collective-permute-start(f32[2,48,192]{2,1,0:T(8,128)S(1)} %pad_maximum_fusion.5), channel_id=1, source_target_pairs={{0,3},{1,2},{2,1},{3,0},{4,7},{5,6},{6,5},{7,4},{8,11},{9,10},{10,... | collective-permute-start | bytes 221192 | tf_op jit(solution)/shard_map/ppermute | solution.py:35
  (11 other events, 49.4 us)
